TPU v7x, 256 devices: a whole 4x4x8 slice. The times are simulated.
256 devices in a mesh: group: 8 (over x, z_lo), member: 32 (over y, z_hi, core).
Axes of the slice: x: 4, y: 4, z: 8 (z_hi: 4, z_lo: 2; z = z_hi * 2 + z_lo), core: 2. Of those that a mesh axis runs over, the one named last changes fastest.
Arguments:
- tokens: bfloat16 [2048, 2048], P(('group', 'member')), may hold values from -6 to 6
- expert_ids: int32 [2048, 8], P('group'), may hold values from 0 to 127, all different within a row
- combine: float32 [2048, 8], P('group'), may hold values from 0.05 to 0.5
- hot_group: int32 [16], replicated, may hold values from 0 to 7
- expert_weights: bfloat16 [256, 2048, 1152], P(('group', 'member')), may hold values from -0.1875 to 0.1875
- out_grad: bfloat16 [2048, 2048], P(('group', 'member')), may hold values from -6 to 6
Outputs:
- mixed_out: bfloat16 [2048, 2048], P(('group', 'member'))
- token_grad: bfloat16 [2048, 2048], P(('group', 'member'))
- weight_grad: bfloat16 [256, 2048, 1152], P(('group', 'member'))
Inputs may be any that keep to these rules, and one draw needn't show every extreme that they name: `expert_ids`: each row names 8 different experts. `hot_group`: entry j names the group whose expert number j + 16 * group is hot.
All inputs are finite; a program needn't handle non-finite values.
Results may differ from a plain program's by a relative error of at most 0.018.
Values may be sent and summed in bfloat16 or wider, within the bound.
A program may use at most 128 MiB of HBM per device.

v0:
```python
import jax
import jax.numpy as jnp
from jax import lax
from jax.sharding import PartitionSpec as P


def broadcast(block, axis, holder):
    block = jnp.where(lax.axis_index(axis) == holder, block, jnp.zeros_like(block))
    return lax.psum(block, axis)


def expert_pass(rows_in, grad_rows, weights):
    half_width = weights.shape[1] // 3
    pre_act = jnp.dot(rows_in, weights[:, : 2 * half_width], preferred_element_type=jnp.float32)
    gate_pre = pre_act[:, :half_width]
    up_pre = pre_act[:, half_width:]
    sigmoid_gate = jax.nn.sigmoid(gate_pre)
    active = gate_pre * sigmoid_gate
    hidden = (active * up_pre).astype(jnp.bfloat16)
    down_w = weights[:, 2 * half_width :]
    partial_value = lax.dot_general(
        hidden, down_w, (((1,), (1,)), ((), ())), preferred_element_type=jnp.float32
    ).astype(jnp.bfloat16)
    d_hidden = jnp.dot(grad_rows, down_w, preferred_element_type=jnp.float32)
    d_gate = d_hidden * up_pre * sigmoid_gate * (1.0 + gate_pre * (1.0 - sigmoid_gate))
    d_up = d_hidden * active
    d_both = jnp.concatenate([d_gate, d_up], axis=1).astype(jnp.bfloat16)
    d_rows = lax.dot_general(
        d_both,
        weights[:, : 2 * half_width],
        (((1,), (1,)), ((), ())),
        preferred_element_type=jnp.float32,
    ).astype(jnp.bfloat16)
    grad_in = lax.dot_general(
        rows_in, d_both, (((0,), (0,)), ((), ())), preferred_element_type=jnp.float32
    )
    grad_out = lax.dot_general(
        grad_rows, hidden, (((0,), (0,)), ((), ())), preferred_element_type=jnp.float32
    )
    return (partial_value, d_rows, jnp.concatenate([grad_in, grad_out], axis=1))


def route_tables(
    expert_ids, combine, hot_group, local_index, groups, per_group, capacity, hot_capacity
):
    owner_group = expert_ids // per_group
    is_local = expert_ids % per_group == local_index
    group_range = jnp.arange(groups, dtype=jnp.int32)
    onehot = is_local[:, :, None] & (owner_group[:, :, None] == group_range)
    hit_count = jnp.sum(onehot.astype(jnp.int32), axis=1)
    weight = jnp.sum(jnp.where(onehot, combine[:, :, None], 0.0), axis=1)
    rank_table = jnp.cumsum(hit_count, axis=0) - hit_count
    hot_owner = hot_group[local_index]
    hot_column = group_range == hot_owner
    cap_limit = jnp.where(hot_column, hot_capacity, capacity)
    kept_slot = (hit_count > 0) & (rank_table < cap_limit)
    positions = jnp.arange(hit_count.shape[0], dtype=jnp.int32)
    send_kept = kept_slot & jnp.logical_not(hot_column)
    slot_range = jnp.arange(capacity, dtype=jnp.int32)
    slot_match = send_kept.T[:, None, :] & (rank_table.T[:, None, :] == slot_range[None, :, None])
    send_token = jnp.sum(jnp.where(slot_match, positions, 0), axis=2)
    send_live = jnp.any(slot_match, axis=2)
    send_weight = jnp.sum(jnp.where(slot_match, weight.T[:, None, :], 0.0), axis=2)
    hot_kept = jnp.any(kept_slot & hot_column, axis=1)
    hot_rank = jnp.sum(jnp.where(hot_column, rank_table, 0), axis=1)
    hot_weight = jnp.sum(jnp.where(hot_column, weight, 0.0), axis=1)
    hot_slots = jnp.arange(hot_capacity, dtype=jnp.int32)
    hot_match = hot_kept[None, :] & (hot_rank[None, :] == hot_slots[:, None])
    hot_token = jnp.sum(jnp.where(hot_match, positions, 0), axis=1)
    hot_live = jnp.any(hot_match, axis=1)
    hot_coeff = jnp.sum(jnp.where(hot_match, hot_weight[None, :], 0.0), axis=1)
    pair_rank = jnp.take_along_axis(rank_table, owner_group, axis=1)
    pair_kept = jnp.take_along_axis(kept_slot, owner_group, axis=1) & is_local
    pair_row = jnp.where(
        owner_group == hot_owner, groups * capacity + pair_rank, owner_group * capacity + pair_rank
    )
    pair_row = jnp.where(pair_kept, pair_row, 0)
    return (
        send_token,
        send_live,
        send_weight,
        hot_token,
        hot_live,
        hot_coeff,
        pair_row,
        pair_kept,
        hot_owner,
    )


def shards(tokens, expert_ids, combine, hot_group, expert_weights, out_grad):
    groups = lax.axis_size("group")
    members = lax.axis_size("member")
    per_group = members // 2
    local_index = lax.axis_index("member") // 2
    my_group = lax.axis_index("group")
    capacity = 24 * tokens.shape[0] // groups
    hot_capacity = 2 * capacity
    model_width = tokens.shape[1]
    weights = expert_weights[0]
    group_tokens, group_grads = (
        lax.all_gather(tokens, "member", axis=0, tiled=True),
        lax.all_gather(out_grad, "member", axis=0, tiled=True),
    )
    (
        send_token,
        send_live,
        send_weight,
        hot_token,
        hot_live,
        hot_coeff,
        pair_row,
        pair_kept,
        hot_owner,
    ) = route_tables(
        expert_ids, combine, hot_group, local_index, groups, per_group, capacity, hot_capacity
    )
    send_rows = jnp.where(
        send_live[..., None], group_tokens[send_token], jnp.zeros((), jnp.bfloat16)
    )
    send_grads = (send_weight[..., None] * group_grads[send_token].astype(jnp.float32)).astype(
        jnp.bfloat16
    )
    hot_rows = jnp.where(hot_live[:, None], group_tokens[hot_token], jnp.zeros((), jnp.bfloat16))
    hot_grads = (hot_coeff[:, None] * group_grads[hot_token].astype(jnp.float32)).astype(
        jnp.bfloat16
    )
    recv_rows, recv_grads = (
        lax.all_to_all(send_rows, "group", split_axis=0, concat_axis=0, tiled=True),
        lax.all_to_all(send_grads, "group", split_axis=0, concat_axis=0, tiled=True),
    )
    part_rows, back_rows, own_grad = expert_pass(
        recv_rows.reshape(groups * capacity, model_width),
        recv_grads.reshape(groups * capacity, model_width),
        weights,
    )
    ret_parts, ret_backs = (
        lax.all_to_all(
            part_rows.reshape(groups, capacity, model_width),
            "group",
            split_axis=0,
            concat_axis=0,
            tiled=True,
        ),
        lax.all_to_all(
            back_rows.reshape(groups, capacity, model_width),
            "group",
            split_axis=0,
            concat_axis=0,
            tiled=True,
        ),
    )
    is_owner = hot_owner == my_group
    shadow = broadcast(expert_weights, "group", hot_owner)[0]
    hot_part, hot_back, shadow_grad = expert_pass(hot_rows, hot_grads, shadow)
    shadow_sum = lax.psum(shadow_grad.astype(jnp.bfloat16), "group").astype(jnp.float32)
    weight_total = own_grad + jnp.where(is_owner, shadow_sum, 0.0)
    results = jnp.concatenate([ret_parts.reshape(groups * capacity, model_width), hot_part], 0)
    backs = jnp.concatenate([ret_backs.reshape(groups * capacity, model_width), hot_back], 0)
    slot_total = results.shape[0]
    slot_index = jnp.arange(slot_total, dtype=jnp.int32)
    coeff_table = jnp.zeros((expert_ids.shape[0], slot_total), jnp.float32)
    live_table = jnp.zeros((expert_ids.shape[0], slot_total), jnp.float32)
    for column in range(expert_ids.shape[1]):
        matched = pair_kept[:, column][:, None] & (
            pair_row[:, column][:, None] == slot_index[None, :]
        )
        coeff_table = coeff_table + jnp.where(matched, combine[:, column][:, None], 0.0)
        live_table = live_table + jnp.where(matched, 1.0, 0.0)
    mixed_term = jnp.dot(coeff_table, results.astype(jnp.float32), precision=lax.Precision.HIGHEST)
    grad_term = jnp.dot(live_table.astype(jnp.bfloat16), backs, preferred_element_type=jnp.float32)
    mixed_out, token_grad = (
        lax.psum_scatter(
            mixed_term.astype(jnp.bfloat16), "member", scatter_dimension=0, tiled=True
        ).astype(jnp.float32),
        lax.psum_scatter(
            grad_term.astype(jnp.bfloat16), "member", scatter_dimension=0, tiled=True
        ).astype(jnp.float32),
    )
    return (
        mixed_out.astype(jnp.bfloat16),
        token_grad.astype(jnp.bfloat16),
        weight_total.astype(jnp.bfloat16)[None],
    )


def solution(mesh):
    return jax.shard_map(
        shards,
        mesh=mesh,
        in_specs=(
            P(("group", "member"), None),
            P("group", None),
            P("group", None),
            P(),
            P(("group", "member"), None, None),
            P(("group", "member"), None),
        ),
        out_specs=(
            P(("group", "member"), None),
            P(("group", "member"), None),
            P(("group", "member"), None, None),
        ),
        check_vma=False,
    )
```

profile of v0, /device:TPU:1, one launch (start us, length us, event | category | flops | bytes accessed | tf_op | source)
XLA Modules:
  0.0 569.2 jit_solution(2118505002514639976)
XLA Ops:
  8.0 0.7 all-gather.3.cloned.1.call-update
  8.8 0.7 all-gather.5.cloned.1.call-update
  9.5 1.2 dynamic_slice.3
  11.4 4.9 select_bitcast_fusion
  16.4 0.7 copy-done.3
  17.1 0.6 reduce-window.6
  18.0 0.7 broadcast_select_fusion.4
  18.6 0.7 iota_compare_fusion.11
  20.4 0.2 fusion.62
  20.6 94.7 %all-gather.3.cloned.1.call-done = bf16[256,2048]{1,0:T(8,128)(2,1)} async-done(((bf16[8,2048]{1,0:T(8,128)(2,1)}), bf16[256,2048]{1,0:T(8,128)(2,1)}) %all-gather.3.cloned.1.call-update) | async-done | bytes 1048592 | tf_op jit(solution)/shard_map/all_gather | solution.py:102
  115.3 3.4 gather_fusion
  118.7 1.0 broadcast_select_fusion
  119.7 4.0 all-to-all-start
  123.8 0.7 gather_fusion.1
  124.5 71.1 %all-gather.5.cloned.1.call-done = bf16[256,2048]{1,0:T(8,128)(2,1)} async-done(((bf16[8,2048]{1,0:T(8,128)(2,1)}), bf16[256,2048]{1,0:T(8,128)(2,1)}) %all-gather.5.cloned.1.call-update) | async-done | bytes 1048592 | tf_op jit(solution)/shard_map/all_gather | solution.py:103
  195.6 2.2 gather_fusion.3
  197.8 44.3 %all-reduce.3.cloned.1.call-done = bf16[2048,1152]{1,0:T(8,128)(2,1)} async-done(((bf16[2048,1152]{1,0:T(8,128)(2,1)}), bf16[2048,1152]{1,0:T(8,128)(2,1)}) %all-reduce.3.cloned.1.call-update) | async-done | bytes 4718608 | tf_op jit(solution)/shard_map/psum | solution.py:9
  242.1 2.6 fusion.4
  244.7 1.8 multiply_convert_fusion.7
  246.5 0.6 convolution_convert_fusion.1
  247.2 1.0 convolution_convert_fusion
  248.2 2.6 pad_maximum_fusion
  250.9 1.1 copy-done
  252.0 1.1 gather_fusion.2
  253.2 1.1 fusion.16
  254.2 4.0 all-to-all-start.2
  258.4 12.5 %gather_fusion.5 = s32[2048]{0:T(1024)S(1)} fusion(s32[256,8]{0,1:T(8,128)S(1)} %get-tuple-element.28, s32[2048]{0:T(1024)S(1)} %reshape.135), kind=kCustom, calls=%fused_computation.5 | custom fusion | bytes 32768 | tf_op jit(solution)/shard_map/jit(take_along_axis)/gather | solution.py:72
  271.0 16.7 %gather_fusion.4 = pred[2048]{0:T(1024)(128)(4,1)S(1)} fusion(pred[256,8]{0,1:T(8,128)(4,1)S(1)} %get-tuple-element.27, s32[2048]{0:T(1024)S(1)} %reshape.135), kind=kCustom, calls=%fused_computation.4 | custom fusion | bytes 20480 | tf_op jit(solution)/shard_map/jit(take_along_axis)/gather | solution.py:73
  288.1 2.7 fusion.8
  290.8 2.3 multiply_convert_fusion.2
  293.1 3.0 convolution_convert_fusion.4
  296.2 5.1 all-to-all-start.1
  301.3 0.7 select_select_fusion
  302.1 4.0 fusion.10
  306.1 2.0 convolution_convert_fusion.5
  308.1 14.6 %all-to-all-done.1 = bf16[8,24,2048]{2,1,0:T(8,128)(2,1)S(1)} async-done(((bf16[8,24,2048]{2,1,0:T(8,128)(2,1)}), bf16[8,24,2048]{2,1,0:T(8,128)(2,1)S(1)}, u32[]{:S(2)}, u32[]{:S(2)}) %all-to-all-start.1) | async-done | bytes 786464 | tf_op jit(solution)/shard_map/all_to_all | solution.py:138
  322.6 3.5 all-to-all-start.3
  326.2 0.2 reduce-scatter.3.cloned.1.call-start
  326.4 2.8 convolution_convert_fusion.3
  329.9 3.7 fusion.63
  333.6 2.9 fusion.13
  336.6 10.6 %all-to-all-done.3 = bf16[8,24,2048]{2,1,0:T(8,128)(2,1)S(1)} async-done(((bf16[8,24,2048]{2,1,0:T(8,128)(2,1)}), bf16[8,24,2048]{2,1,0:T(8,128)(2,1)S(1)}, u32[]{:S(2)}, u32[]{:S(2)}) %all-to-all-start.3) | async-done | bytes 786464 | tf_op jit(solution)/shard_map/all_to_all | solution.py:145
  347.2 2.0 convolution_convert_fusion.2
  349.2 1.8 fusion.131
  350.9 133.2 %all-reduce.5.cloned.1.call-done = bf16[2048,1152]{0,1:T(8,128)(2,1)} async-done(((bf16[2048,1152]{0,1:T(8,128)(2,1)}), bf16[2048,1152]{0,1:T(8,128)(2,1)}) %all-reduce.5.cloned.1.call-update) | async-done | bytes 4718608 | tf_op jit(solution)/shard_map/psum | solution.py:156
  484.1 8.4 %fusion.1 = bf16[1,2048,1152]{1,2,0:T(8,128)(2,1)} fusion(bf16[2048,1152]{0,1:T(8,128)(2,1)} %all-reduce.5.cloned.1.call-done, f32[2048,384]{0,1:T(8,128)S(1)} %fusion.131, f32[2048,768]{0,1:T(8,128)} %fusion.63, pred[]{:T(512)S(6)} %eq.243), kind=kLoop, calls=%fused_computation.8 | loop fusion | flops 11796480 | bytes 18874368 | tf_op jit(solution)/shard_map/broadcast_in_dim | solution.py:183
  492.5 6.6 %copy.23 = bf16[1,2048,1152]{2,1,0:T(8,128)(2,1)} copy(bf16[1,2048,1152]{1,2,0:T(8,128)(2,1)} %fusion.1) | data formatting | bytes 9437184
  499.2 62.9 %reduce-scatter.5.cloned.1.call-done = bf16[8,2048]{1,0:T(8,128)(2,1)} async-done(((bf16[256,2048]{1,0:T(8,128)(2,1)}), bf16[8,2048]{1,0:T(8,128)(2,1)}) %reduce-scatter.5.cloned.1.call-update) | async-done | bytes 32784 | tf_op jit(solution)/shard_map/reduce_scatter | solution.py:176
  (50 shorter events, 2.4 us)
Async XLA Ops:
  8.0 107.3 %all-gather.3.cloned.1.call-start = ((), (), s32[]{:S(2)}) async-start(), calls=%async_computation.6 | async-start | bytes 1081344 | tf_op jit(solution)/shard_map/all_gather | solution.py:102
  8.7 186.9 %all-gather.5.cloned.1.call-start = ((), (), s32[]{:S(2)}) async-start(), calls=%async_computation.9 | async-start | bytes 1081344 | tf_op jit(solution)/shard_map/all_gather | solution.py:103
  9.5 232.6 %all-reduce.3.cloned.1.call-start = ((), (), s32[]{:S(2)}) async-start(), calls=%async_computation.7 | async-start | bytes 9437184 | tf_op jit(solution)/shard_map/psum | solution.py:9
  16.4 0.7 copy-start.3
  16.4 3.8 copy-start.4
  115.3 8.4 %copy-start.1 = (bf16[256,2048]{1,0:T(8,128)(2,1)S(1)}, bf16[256,2048]{1,0:T(8,128)(2,1)}, u32[]{:S(2)}) copy-start(bf16[256,2048]{1,0:T(8,128)(2,1)} %all-gather.3.cloned.1.call-done) | copy-start | bytes 3145732
  119.7 134.5 %all-to-all-start = ((bf16[8,24,2048]{2,1,0:T(8,128)(2,1)}), bf16[8,24,2048]{2,1,0:T(8,128)(2,1)S(1)}, u32[]{:S(2)}, u32[]{:S(2)}) async-start(bf16[8,24,2048]{2,1,0:T(8,128)(2,1)} %broadcast_select_fusion), calls=%async_computation | async-start | bytes 1572864 | tf_op jit(solution)/shard_map/all_to_all | solution.py:129
  123.7 360.4 %all-reduce.5.cloned.1.call-start = ((), (), s32[]{:S(2)}) async-start(), calls=%async_computation.11 | async-start | bytes 9437184 | tf_op jit(solution)/shard_map/psum | solution.py:156
  250.8 1.2 copy-start
  254.2 36.5 %all-to-all-start.2 = ((bf16[8,24,2048]{2,1,0:T(8,128)(2,1)}), bf16[8,24,2048]{2,1,0:T(8,128)(2,1)S(1)}, u32[]{:S(2)}, u32[]{:S(2)}) async-start(bf16[8,24,2048]{2,1,0:T(8,128)(2,1)} %fusion.16), calls=%async_computation.3 | async-start | bytes 1572864 | tf_op jit(solution)/shard_map/all_to_all | solution.py:130
  290.8 15.3 %copy-start.2 = (bf16[8,24,2048]{2,1,0:T(8,128)(2,1)}, bf16[8,24,2048]{2,1,0:T(8,128)(2,1)S(1)}, u32[]{:S(2)}) copy-start(bf16[8,24,2048]{2,1,0:T(8,128)(2,1)S(1)} %all-to-all-done.2) | copy-start | bytes 2359300
  296.2 26.5 %all-to-all-start.1 = ((bf16[8,24,2048]{2,1,0:T(8,128)(2,1)}), bf16[8,24,2048]{2,1,0:T(8,128)(2,1)S(1)}, u32[]{:S(2)}, u32[]{:S(2)}) async-start(bf16[8,24,2048]{2,1,0:T(8,128)(2,1)} %bitcast.26), calls=%async_computation.1 | async-start | bytes 1572864 | tf_op jit(solution)/shard_map/all_to_all | solution.py:138
  322.6 24.5 %all-to-all-start.3 = ((bf16[8,24,2048]{2,1,0:T(8,128)(2,1)}), bf16[8,24,2048]{2,1,0:T(8,128)(2,1)S(1)}, u32[]{:S(2)}, u32[]{:S(2)}) async-start(bf16[8,24,2048]{2,1,0:T(8,128)(2,1)} %bitcast.34), calls=%async_computation.4 | async-start | bytes 1572864 | tf_op jit(solution)/shard_map/all_to_all | solution.py:145
  326.2 173.0 %reduce-scatter.3.cloned.1.call-start = ((), (), s32[]{:S(2)}) async-start(), calls=%async_computation.8 | async-start | bytes 1081344 | tf_op jit(solution)/shard_map/reduce_scatter | solution.py:173
  329.2 232.8 %reduce-scatter.5.cloned.1.call-start = ((), (), s32[]{:S(2)}) async-start(), calls=%async_computation.10 | async-start | bytes 1081344 | tf_op jit(solution)/shard_map/reduce_scatter | solution.py:176
Sparse Core Ops, SparseCore 0:
  11.4 103.9 all-gather.2
  117.9 77.6 all-gather.4
  331.4 136.7 reduce-scatter.2
  472.8 89.1 reduce-scatter.4
Sparse Core Ops, SparseCore 1:
  16.5 225.6 all-reduce.2
  250.9 233.2 all-reduce.4
where the time goes:
time: 571 us; the launch traced here: 569 us
  waiting for transfers between devices  433 us (76%)
  local copies, waits for them, and re-layouts  47.2 us (8%)
  matrix products  33.3 us (6%)
  other arithmetic  22 us (4%)
  starting transfers between devices  17.1 us (3%)
  between operations  16.8 us (3%)
    psum x1, waiting for transfers between devices, shards(): lax.psum(shadow_grad.astype(jnp.bfloat16), 'group').astype(jnp.float32)  133 us
    all_gather x1, waiting for transfers between devices, shards(): lax.all_gather(tokens, 'member', axis=0, tiled=True)  94.7 us
    all_gather x1, waiting for transfers between devices, shards(): lax.all_gather(out_grad, 'member', axis=0, tiled=True)  71.1 us
    reduce_scatter x1, waiting for transfers between devices, shards(): lax.psum_scatter(grad_term.astype(jnp.bfloat16), 'member', scatter_dimens...  62.9 us
    psum x1, waiting for transfers between devices, broadcast(): return lax.psum(block, axis)  44.3 us
    gather x5, local copies, waits for them, and re-layouts, route_tables(): pair_kept = jnp.take_along_axis(kept_slot, owner_group, axis=1) & is_local  17.1 us
    all_to_all x1, waiting for transfers between devices, shards(): lax.all_to_all(part_rows.reshape(groups, capacity, model_width), 'group',...  14.6 us
    gather x3, local copies, waits for them, and re-layouts, route_tables(): pair_rank = jnp.take_along_axis(rank_table, owner_group, axis=1)  12.7 us
  transfers between devices with their start and end apart: 10, of which 7 were waited for; matrix products, arithmetic and copies ran while one was open for 18% of the time, Pallas kernels for 0%

commit v1 on v0

v1 whole, which is shorter than its diff:
```python
import functools

import jax
import jax.numpy as jnp
from jax import lax
from jax.experimental import pallas as pl
from jax.experimental.pallas import tpu as pltpu
from jax.sharding import PartitionSpec as P

MESH = pl.DeviceIdType.MESH
F32 = jnp.float32
BF16 = jnp.bfloat16
CAP = 24
HOT_CAP = 48
CHUNKS = 4


def wait(ref, sem):
    pltpu.make_async_copy(ref, ref, sem).wait()


def dot(a, b, dims):
    return lax.dot_general(a, b, (dims, ((), ())), preferred_element_type=F32)


def layer(
    groups, ny, nz,
    hot_ref, table_ref, tok_ref, grad_ref, w_hbm,
    out_ref, wg_hbm,
    w, buf, send, rows, pick, scale, spread, acc, hid, dab,
    pair, other, total, ret, res, yrecv, ysum, zrecv, fin, wg,
    w_sem, z_send, z_recv, y_send, y_recv, g_send, g_recv, f_send, f_recv,
    h_send, h_recv, r_send, r_recv, ry_send, ry_recv, rz_send, rz_recv,
    o_send, o_recv, wg_sem,
):
    chunks, _, _, width = buf.shape
    tokens = table_ref.shape[1]
    top = table_ref.shape[0] // 2
    slots = groups * HOT_CAP
    half = hid.shape[1]
    my_group = lax.axis_index("group")
    member = lax.axis_index("member")
    core = member % 2
    local = member // 2
    z = local % nz
    y = local // nz
    partner = (my_group, member + 1 - 2 * core)

    def z_peer(step, kind):
        return (my_group, (y * nz + (z + step) % nz) * 2 + kind)

    def y_peer(step):
        return (my_group, (((y + step) % ny) * nz + z) * 2 + core)

    def g_peer(step):
        return ((my_group + step) % groups, member)

    w_copy = pltpu.make_async_copy(w_hbm.at[0], w, w_sem)
    w_copy.start()

    barrier = pltpu.get_barrier_semaphore()
    peers = [partner]
    peers += [z_peer(s, k) for s in range(1, nz) for k in range(2)]
    peers += [y_peer(s) for s in range(1, ny)]
    peers += [g_peer(s) for s in range(1, groups)]
    for peer in peers:
        pl.semaphore_signal(barrier, inc=1, device_id=peer, device_id_type=MESH)
    pl.semaphore_wait(barrier, len(peers))

    def push(src, dst, send_sem, recv_sem, peer):
        pltpu.make_async_remote_copy(
            src_ref=src, dst_ref=dst, send_sem=send_sem, recv_sem=recv_sem,
            device_id=peer, device_id_type=MESH,
        ).start()

    for ch in range(chunks):
        cols = pl.ds(ch * width, width)
        place = buf.at[ch, member]
        sources = (tok_ref.at[:, cols], grad_ref.at[:, cols])
        for step in range(1, nz):
            for kind in range(2):
                push(sources[kind], place, z_send.at[ch], z_recv.at[ch], z_peer(step, kind))
        for kind in range(2):

            @pl.when(core == kind)
            def _():
                pltpu.make_async_copy(sources[kind], place, z_recv.at[ch]).start()
                push(sources[1 - kind], place, z_send.at[ch], z_recv.at[ch], partner)

    ids = table_ref[0:top, :]
    weights = table_ref[top : 2 * top, :]
    group_row = lax.broadcasted_iota(jnp.int32, (groups, tokens), 0)
    wanted = (group_row * (ny * nz) + local).astype(F32)
    hit = jnp.zeros((groups, tokens), F32)
    weight = jnp.zeros((groups, tokens), F32)
    for k in range(top):
        match = ids[k : k + 1, :] == wanted
        hit = hit + jnp.where(match, 1.0, 0.0)
        weight = weight + jnp.where(match, weights[k : k + 1, :], 0.0)
    before = lax.broadcasted_iota(jnp.int32, (tokens, tokens), 0) < lax.broadcasted_iota(
        jnp.int32, (tokens, tokens), 1
    )
    earlier = jnp.where(before, 1.0, 0.0).astype(BF16)
    rank = dot(hit.astype(BF16), earlier, ((1,), (0,)))
    limit = jnp.where(group_row == hot_ref[local], float(HOT_CAP), float(CAP))
    kept = (hit > 0.0) & (rank < limit)
    rank = jnp.where(kept, rank, -1.0)
    is_rows = core == 0
    gather_weight = jnp.where(is_rows, 1.0, weight)
    spread_weight = jnp.where(is_rows, weight, 1.0)
    slot = lax.broadcasted_iota(jnp.int32, (HOT_CAP, tokens), 0).astype(F32)
    for g in range(groups):
        at = pl.ds(g * HOT_CAP, HOT_CAP)
        one = jnp.where(rank[g : g + 1, :] == slot, 1.0, 0.0)
        pick[at, :] = one.astype(BF16)
        scale[at, :] = jnp.broadcast_to(
            jnp.sum(one * gather_weight[g : g + 1, :], axis=1, keepdims=True), (HOT_CAP, 128)
        )
        acc[at, 0:tokens] = one * spread_weight[g : g + 1, :]
    turned = acc[:, 0:tokens].T
    spread[0] = turned.astype(BF16)
    spread[1] = (turned - turned.astype(BF16).astype(F32)).astype(BF16)

    def to_y(ch):
        mine = pl.ds(y * nz * 2, nz * 2)
        wait(buf.at[ch, mine], z_recv.at[ch])
        for step in range(1, ny):
            push(buf.at[ch, mine], buf.at[ch, mine], y_send.at[ch], y_recv.at[ch], y_peer(step))

    def to_owner(ch):
        wait(buf.at[ch, pl.ds(0, (ny - 1) * nz * 2)], y_recv.at[ch])
        block = buf[ch].astype(F32).reshape(tokens, width).astype(BF16)
        picked = dot(pick[...], block, ((1,), (0,))) * scale[:, 0:1]
        send[ch] = picked.astype(BF16).reshape(groups, HOT_CAP, width)
        for step in range(1, groups):
            peer = g_peer(step)
            push(send.at[ch, peer[0]], rows.at[core, ch, my_group], g_send.at[ch], g_recv.at[ch], peer)
        pltpu.make_async_copy(
            send.at[ch, my_group], rows.at[core, ch, my_group], g_recv.at[ch]
        ).start()

    def to_partner(ch):
        wait(rows.at[core, ch], g_recv.at[ch])
        push(rows.at[core, ch], rows.at[core, ch], f_send.at[ch], f_recv.at[ch], partner)

    def accumulate(ch):
        wait(rows.at[1 - core, ch], f_recv.at[ch])
        if ch == 0:
            w_copy.wait()
        at = pl.ds(ch * width, width)
        pre = dot(rows[0, ch].reshape(slots, width), w[at, 0 : 2 * half], ((1,), (0,)))
        down = dot(rows[1, ch].reshape(slots, width), w[at, 2 * half :], ((1,), (0,)))
        if ch == 0:
            acc[:, 0 : 2 * half] = pre
            acc[:, 2 * half :] = down
        else:
            acc[:, 0 : 2 * half] += pre
            acc[:, 2 * half :] += down

    for step in range(chunks + 3):
        for lag, phase in enumerate((to_y, to_owner, to_partner, accumulate)):
            if 0 <= step - lag < chunks:
                phase(step - lag)

    @pl.loop(0, groups)
    def _(g):
        at = pl.ds(pl.multiple_of(g * HOT_CAP, HOT_CAP), HOT_CAP)
        gate = acc[at, 0:half]
        up = acc[at, half : 2 * half]
        d_hidden = acc[at, 2 * half :]
        sig = jax.nn.sigmoid(gate)
        active = gate * sig
        hid[at, :] = (active * up).astype(BF16)
        dab[at, 0:half] = (d_hidden * up * sig * (1.0 + gate * (1.0 - sig))).astype(BF16)
        dab[at, half:] = (d_hidden * active).astype(BF16)

    def results(ch):
        at = pl.ds(ch * width, width)
        part = dot(hid[...], w[at, 2 * half :], ((1,), (1,)))
        back = dot(dab[...], w[at, 0 : 2 * half], ((1,), (1,)))
        pair[0, ch] = part.astype(BF16).reshape(groups, HOT_CAP, width)
        pair[1, ch] = back.astype(BF16).reshape(groups, HOT_CAP, width)
        push(pair.at[1 - core, ch], other.at[ch], h_send.at[ch], h_recv.at[ch], partner)

    def to_origin(ch):
        wait(other.at[ch], h_recv.at[ch])
        total[ch] = (pair[core, ch].astype(F32) + other[ch].astype(F32)).astype(BF16)
        for step in range(1, groups):
            peer = g_peer(step)
            push(total.at[ch, peer[0]], ret.at[ch, my_group], r_send.at[ch], r_recv.at[ch], peer)
        pltpu.make_async_copy(total.at[ch, my_group], ret.at[ch, my_group], r_recv.at[ch]).start()

    def weight_part(ch):
        at = pl.ds(ch * width, width)
        wg[at, 0 : 2 * half] = dot(
            rows[0, ch].reshape(slots, width), dab[...], ((0,), (0,))
        ).astype(BF16)
        wg[at, 2 * half :] = dot(
            rows[1, ch].reshape(slots, width), hid[...], ((0,), (0,))
        ).astype(BF16)
        pltpu.make_async_copy(wg.at[at], wg_hbm.at[0, at], wg_sem.at[ch]).start()

    def back_y(ch):
        wait(ret.at[ch], r_recv.at[ch])
        got = ret[ch].reshape(slots, width)
        mixed = dot(spread[0], got, ((1,), (0,))) + dot(spread[1], got, ((1,), (0,)))
        res[ch] = mixed.astype(BF16).reshape(ny, nz, 16, width)
        for step in range(1, ny):
            push(
                res.at[ch, (y + step) % ny], yrecv.at[ch, y], ry_send.at[ch], ry_recv.at[ch],
                y_peer(step),
            )
        pltpu.make_async_copy(res.at[ch, y], yrecv.at[ch, y], ry_recv.at[ch]).start()

    def back_z(ch):
        wait(yrecv.at[ch], ry_recv.at[ch])
        ysum[ch] = jnp.sum(yrecv[ch].astype(F32), axis=0).astype(BF16)
        for step in range(1, nz):
            push(
                ysum.at[ch, (z + step) % nz], zrecv.at[ch, z], rz_send.at[ch], rz_recv.at[ch],
                z_peer(step, core),
            )
        pltpu.make_async_copy(ysum.at[ch, z], zrecv.at[ch, z], rz_recv.at[ch]).start()

    def finish(ch):
        wait(zrecv.at[ch], rz_recv.at[ch])
        done = jnp.sum(zrecv[ch].astype(F32), axis=0)
        fin[ch] = done.reshape(2, 8, width).astype(BF16)
        place = out_ref.at[core, ch]
        push(fin.at[ch, 1 - core], place, o_send.at[ch], o_recv.at[ch], partner)
        pltpu.make_async_copy(fin.at[ch, core], place, o_recv.at[ch]).start()

    phases = (results, to_origin, weight_part, back_y, back_z, finish)
    for step in range(chunks + len(phases) - 1):
        for lag, phase in enumerate(phases):
            if 0 <= step - lag < chunks:
                phase(step - lag)

    for ch in range(chunks):
        at = pl.ds(ch * width, width)
        pltpu.make_async_copy(wg.at[at], wg_hbm.at[0, at], wg_sem.at[ch]).wait()
        wait(buf.at[ch, pl.ds(0, 2 * nz - 1)], z_send.at[ch])
        wait(buf.at[ch, pl.ds(0, (ny - 1) * nz * 2)], y_send.at[ch])
        wait(send.at[ch, pl.ds(0, groups - 1)], g_send.at[ch])
        wait(rows.at[core, ch], f_send.at[ch])
        wait(pair.at[1 - core, ch], h_send.at[ch])
        wait(total.at[ch, pl.ds(0, groups - 1)], r_send.at[ch])
        wait(res.at[ch, pl.ds(0, ny - 1)], ry_send.at[ch])
        wait(ysum.at[ch, pl.ds(0, nz - 1)], rz_send.at[ch])
        wait(fin.at[ch, 1 - core], o_send.at[ch])
        wait(fin.at[ch], o_recv.at[ch])


def shards(ny, nz, tokens, expert_ids, combine, hot_group, expert_weights, out_grad):
    groups = lax.axis_size("group")
    chips = ny * nz
    rows_here, model_width = tokens.shape
    group_len = expert_ids.shape[0]
    hidden3 = expert_weights.shape[2]
    half = hidden3 // 3
    width = model_width // CHUNKS
    slots = groups * HOT_CAP
    table = jnp.concatenate([expert_ids.astype(F32).T, combine.T], axis=0)
    dma = pltpu.SemaphoreType.DMA
    block = (CHUNKS, groups, HOT_CAP, width)
    any_space = pl.BlockSpec(memory_space=pl.ANY)
    out, weight_grad = pl.pallas_call(
        functools.partial(layer, groups, ny, nz),
        out_shape=(
            jax.ShapeDtypeStruct((2, CHUNKS, rows_here, width), BF16),
            jax.ShapeDtypeStruct(expert_weights.shape, BF16),
        ),
        in_specs=[
            pl.BlockSpec(memory_space=pltpu.SMEM),
            pl.BlockSpec(memory_space=pltpu.VMEM),
            any_space,
            any_space,
            any_space,
        ],
        out_specs=(pl.BlockSpec(memory_space=pltpu.VMEM), any_space),
        scratch_shapes=[
            pltpu.VMEM((model_width, hidden3), BF16),
            pltpu.VMEM((CHUNKS, 2 * chips, rows_here, width), BF16),
            pltpu.VMEM(block, BF16),
            pltpu.VMEM((2,) + block, BF16),
            pltpu.VMEM((slots, group_len), BF16),
            pltpu.VMEM((slots, 128), F32),
            pltpu.VMEM((2, group_len, slots), BF16),
            pltpu.VMEM((slots, hidden3), F32),
            pltpu.VMEM((slots, half), BF16),
            pltpu.VMEM((slots, 2 * half), BF16),
            pltpu.VMEM((2,) + block, BF16),
            pltpu.VMEM(block, BF16),
            pltpu.VMEM(block, BF16),
            pltpu.VMEM(block, BF16),
            pltpu.VMEM((CHUNKS, ny, nz, 16, width), BF16),
            pltpu.VMEM((CHUNKS, ny, nz, 16, width), BF16),
            pltpu.VMEM((CHUNKS, nz, 16, width), BF16),
            pltpu.VMEM((CHUNKS, nz, 16, width), BF16),
            pltpu.VMEM((CHUNKS, 2, rows_here, width), BF16),
            pltpu.VMEM((model_width, hidden3), BF16),
            dma,
        ]
        + [dma((CHUNKS,))] * 19,
        compiler_params=pltpu.CompilerParams(
            collective_id=0, has_side_effects=True, vmem_limit_bytes=56 * 2**20
        ),
        cost_estimate=pl.CostEstimate(
            flops=6 * slots * model_width * hidden3, bytes_accessed=4 * model_width * hidden3,
            transcendentals=slots * half,
        ),
    )(hot_group, table, tokens, out_grad, expert_weights)
    out = out.transpose(0, 2, 1, 3).reshape(2, rows_here, model_width)
    return out[0], out[1], weight_grad


def solution(mesh):
    nz = 4 if mesh.shape["member"] == 32 else 2
    ny = mesh.shape["member"] // (2 * nz)
    return jax.shard_map(
        functools.partial(shards, ny, nz),
        mesh=mesh,
        in_specs=(
            P(("group", "member"), None),
            P("group", None),
            P("group", None),
            P(),
            P(("group", "member"), None, None),
            P(("group", "member"), None),
        ),
        out_specs=(
            P(("group", "member"), None),
            P(("group", "member"), None),
            P(("group", "member"), None, None),
        ),
        check_vma=False,
    )
```

time: 571 us -> 90.5 us (0.16)
  waiting for transfers between devices: 433 us -> 0 us
  Pallas kernels: 0 us -> 81.3 us
  local copies, waits for them, and re-layouts: 47.2 us -> 6.29 us
  matrix products: 33.3 us -> 0 us
  other arithmetic: 22 us -> 2 us
  starting transfers between devices: 17.1 us -> 0 us
  between operations: 16.8 us -> 0.64 us
    psum x2 -> x0, waiting for transfers between devices: 177 us -> none  [the longest x1 133 us: shards(): lax.psum(shadow_grad.astype(jnp.bfloat16), 'group').astype(jnp.float32)]
    all_gather x2 -> x0, waiting for transfers between devices: 166 us -> none  [the longest x1 94.7 us: shards(): lax.all_gather(tokens, 'member', axis=0, tiled=True)]
    pallas_call x0 -> x1, Pallas kernels: none -> 81.3 us  [shards(): pl.pallas_call(functools.partial(layer, groups, ny, nz), out_shape=(jax.S...]
    reduce_scatter x2 -> x0, waiting for transfers between devices: 62.9 us -> none  [the longest x1 62.9 us: shards(): lax.psum_scatter(grad_term.astype(jnp.bfloat16), 'member', scatter_dimens...]
    gather x12 -> x0, local copies, waits for them, and re-layouts: 37.2 us -> none  [the longest x5 17.1 us: route_tables(): pair_kept = jnp.take_along_axis(kept_slot, owner_group, axis=1) & is_local]
    dot_general x14 -> x0, matrix products: 33.3 us -> none  [the longest x2 6.92 us: expert_pass(): lax.dot_general(d_both, weights[:, :2 * half_width], (((1,), (1,)), ((),...]
    all_to_all x4 -> x0, waiting for transfers between devices: 25.2 us -> none  [the longest x1 14.6 us: shards(): lax.all_to_all(part_rows.reshape(groups, capacity, model_width), 'group',...]
    all_to_all x4 -> x0, starting transfers between devices: 16.6 us -> none  [the longest x1 5.15 us: shards(): lax.all_to_all(part_rows.reshape(groups, capacity, model_width), 'group',...]
  transfers between devices with their start and end apart: 10 -> 0, of which waited for: 7 -> 0; matrix products, arithmetic and copies ran while one was open for 18% -> 0% of each run, Pallas kernels for 0% -> 0%
where the time goes in v1:
time: 90.5 us; the launch traced here: 90.2 us
  Pallas kernels  81.3 us (90%)
  local copies, waits for them, and re-layouts  6.29 us (7%)
  other arithmetic  2 us (2%)
    pallas_call x1, Pallas kernels, shards(): pl.pallas_call(functools.partial(layer, groups, ny, nz), out_shape=(jax.S...  81.3 us
    unnamed x1, local copies, waits for them, and re-layouts  4.88 us

profile of v1, /device:TPU:1, one launch (start us, length us, event | category | flops | bytes accessed | tf_op | source)
XLA Modules:
  0.0 90.2 jit_solution(7226703771738251698)
XLA Ops:
  0.6 0.7 convert_bitcast_fusion
  1.3 1.3 %pad_maximum_fusion.table_ref = f32[16,256]{1,0:T(8,128)} fusion(f32[8,256]{1,0:T(8,128)} %bitcast.9, f32[8,256]{1,0:T(8,128)S(1)} %convert_bitcast_fusion), kind=kLoop, calls=%fused_computation | loop fusion | flops 4096 | bytes 32768 | tf_op jit(solution)/shard_map/concatenate | solution.py:263
  2.6 81.3 %shard_map.85 = (bf16[2,4,8,512]{3,2,1,0:T(8,128)(2,1)}, bf16[1,2048,1152]{2,1,0:T(8,128)(2,1)}) custom-call(s32[16]{0:T(128)} %hot_ref.1, f32[16,256]{1,0:T(8,128)} %pad_maximum_fusion.table_ref, bf16[8,2048]{1,0:T(8,128)(2,1)} %tok_ref.1, bf16[8,2048]{1,0:T(8,128)(2,1)} %grad_ref.1, bf16[1,2048,1152]{2,1,0:T(8,128)(2,1)} %w_hbm.1), custom_call_target="tpu_custom_call" | custom-call | flops 5435817984 | bytes 9437184 | tf_op jit(solution)/shard_map/pallas_call | solution.py:267
  83.9 1.4 %fusion = (bf16[1,8,4,512]{3,1,2,0:T(8,128)(2,1)}, bf16[1,8,4,512]{3,1,2,0:T(8,128)(2,1)}) fusion(bf16[2,8,4,512]{3,1,2,0:T(8,128)(2,1)} %bitcast.6), kind=kLoop, calls=%fused_computation.2 | loop fusion | bytes 131072 | tf_op jit(solution)/shard_map/slice | solution.py:314
  85.3 4.9 %copy.10 = bf16[1,2048,1152]{2,1,0:T(8,128)(2,1)} copy(bf16[1,2048,1152]{2,1,0:T(8,128)(2,1)} %get-tuple-element.14) | data formatting | bytes 9437184

commit v2 on v1

v2 whole, which is shorter than its diff:
```python
import functools

import jax
import jax.numpy as jnp
from jax import lax
from jax.experimental import pallas as pl
from jax.experimental.pallas import tpu as pltpu
from jax.sharding import PartitionSpec as P

MESH = pl.DeviceIdType.MESH
F32 = jnp.float32
BF16 = jnp.bfloat16
CAP = 24
HOT_CAP = 48
VMEM_BYTES = 56 * 2**20
Z_CUTS = (256, 512, 1280)
IN_CUTS = (256, 512, 768, 512)
OUT_CUTS = (256, 512, 512, 512, 256)


def spans(cuts, width):
    whole = sum(cuts)
    ends = [sum(cuts[: i + 1]) * width // whole for i in range(len(cuts))]
    return [(a, b) for a, b in zip([0] + ends[:-1], ends)]


def wait(ref, sem):
    pltpu.make_async_copy(ref, ref, sem).wait()


def dot(a, b, dims):
    return lax.dot_general(a, b, (dims, ((), ())), preferred_element_type=F32)


def layer(
    groups, ny, nz,
    hot_ref, ids_ref, weights_ref, tok_ref, grad_ref, w_hbm,
    out_ref, wg,
    w, buf, send, rows, pick, scale, spread, acc, hid, dab,
    pair, other, total, ret, res, yrecv, ysum, zrecv, fin,
    w_sem, z_send, z_recv, y_send, y_recv, g_send, g_recv, f_send, f_recv,
    h_send, h_recv, r_send, r_recv, ry_send, ry_recv, rz_send, rz_recv,
    o_send, o_recv,
):
    model_width = tok_ref.shape[1]
    z_spans = spans(Z_CUTS, model_width)
    in_spans = spans(IN_CUTS, model_width)
    out_spans = spans(OUT_CUTS, model_width)
    top, tokens = ids_ref.shape
    slots = groups * HOT_CAP
    half = hid.shape[1]
    my_group = lax.axis_index("group")
    member = lax.axis_index("member")
    core = member % 2
    local = member // 2
    z = local % nz
    y = local // nz
    partner = (my_group, member + 1 - 2 * core)

    def z_peer(step, kind):
        return (my_group, (y * nz + (z + step) % nz) * 2 + kind)

    def y_peer(step):
        return (my_group, (((y + step) % ny) * nz + z) * 2 + core)

    def g_peer(step):
        return ((my_group + step) % groups, member)

    w_copy = pltpu.make_async_copy(w_hbm.at[0], w, w_sem)
    w_copy.start()

    barrier = pltpu.get_barrier_semaphore()
    peers = [partner]
    peers += [z_peer(s, k) for s in range(1, nz) for k in range(2)]
    peers += [y_peer(s) for s in range(1, ny)]
    peers += [g_peer(s) for s in range(1, groups)]
    for peer in peers:
        pl.semaphore_signal(barrier, inc=1, device_id=peer, device_id_type=MESH)
    pl.semaphore_wait(barrier, len(peers))

    def push(src, dst, send_sem, recv_sem, peer):
        pltpu.make_async_remote_copy(
            src_ref=src, dst_ref=dst, send_sem=send_sem, recv_sem=recv_sem,
            device_id=peer, device_id_type=MESH,
        ).start()

    def columns(span):
        return pl.ds(span[0], span[1] - span[0])

    for ch, span in enumerate(z_spans):
        cols = columns(span)
        place = buf.at[member, :, cols]
        sources = (tok_ref.at[:, cols], grad_ref.at[:, cols])
        for step in range(1, nz):
            for kind in range(2):
                push(sources[kind], place, z_send.at[ch], z_recv.at[ch], z_peer(step, kind))
        for kind in range(2):

            @pl.when(core == kind)
            def _():
                pltpu.make_async_copy(sources[kind], place, z_recv.at[ch]).start()
                push(sources[1 - kind], place, z_send.at[ch], z_recv.at[ch], partner)

    ids = ids_ref[...]
    weights = weights_ref[...]
    group_row = lax.broadcasted_iota(jnp.int32, (groups, tokens), 0)
    wanted = group_row * (ny * nz) + local
    hit = jnp.zeros((groups, tokens), F32)
    weight = jnp.zeros((groups, tokens), F32)
    for k in range(top):
        match = ids[k : k + 1, :] == wanted
        hit = hit + jnp.where(match, 1.0, 0.0)
        weight = weight + jnp.where(match, weights[k : k + 1, :], 0.0)
    before = lax.broadcasted_iota(jnp.int32, (tokens, tokens), 0) < lax.broadcasted_iota(
        jnp.int32, (tokens, tokens), 1
    )
    earlier = jnp.where(before, 1.0, 0.0).astype(BF16)
    rank = dot(hit.astype(BF16), earlier, ((1,), (0,)))
    limit = jnp.where(group_row == hot_ref[local], float(HOT_CAP), float(CAP))
    kept = (hit > 0.0) & (rank < limit)
    rank = jnp.where(kept, rank, -1.0)
    is_rows = core == 0
    gather_weight = jnp.where(is_rows, 1.0, weight)
    spread_weight = jnp.where(is_rows, weight, 1.0)
    slot = lax.broadcasted_iota(jnp.int32, (HOT_CAP, tokens), 0).astype(F32)
    for g in range(groups):
        at = pl.ds(g * HOT_CAP, HOT_CAP)
        one = jnp.where(rank[g : g + 1, :] == slot, 1.0, 0.0)
        pick[at, :] = one.astype(BF16)
        scale[at, :] = jnp.broadcast_to(
            jnp.sum(one * gather_weight[g : g + 1, :], axis=1, keepdims=True), (HOT_CAP, 128)
        )
        acc[at, 0:tokens] = one * spread_weight[g : g + 1, :]
    turned = acc[:, 0:tokens].T
    spread[0] = turned.astype(BF16)
    spread[1] = (turned - turned.astype(BF16).astype(F32)).astype(BF16)

    def to_y(ch):
        mine = pl.ds(y * nz * 2, nz * 2)
        first, last = in_spans[ch]
        for zc, (a, b) in enumerate(z_spans):
            if first < b <= last or (a < last <= b and b > last):
                if zc not in z_done:
                    z_done.append(zc)
                    wait(buf.at[mine, :, columns((a, b))], z_recv.at[zc])
        block = buf.at[mine, :, columns(in_spans[ch])]
        for step in range(1, ny):
            push(block, block, y_send.at[ch], y_recv.at[ch], y_peer(step))

    def to_owner(ch):
        cols = columns(in_spans[ch])
        wait(buf.at[pl.ds(0, (ny - 1) * nz * 2), :, cols], y_recv.at[ch])
        width = cols.size
        block = buf[:, :, cols].astype(F32).reshape(tokens, width).astype(BF16)
        picked = dot(pick[...], block, ((1,), (0,))) * scale[:, 0:1]
        send[:, :, cols] = picked.astype(BF16).reshape(groups, HOT_CAP, width)
        place = rows.at[core, my_group, :, cols]
        for step in range(1, groups):
            peer = g_peer(step)
            push(send.at[peer[0], :, cols], place, g_send.at[ch], g_recv.at[ch], peer)
        pltpu.make_async_copy(send.at[my_group, :, cols], place, g_recv.at[ch]).start()

    def to_partner(ch):
        block = rows.at[core, :, :, columns(in_spans[ch])]
        wait(block, g_recv.at[ch])
        push(block, block, f_send.at[ch], f_recv.at[ch], partner)

    def accumulate(ch):
        at = columns(in_spans[ch])
        wait(rows.at[1 - core, :, :, at], f_recv.at[ch])
        if ch == 0:
            w_copy.wait()
        pre = dot(rows[0, :, :, at].reshape(slots, at.size), w[at, 0 : 2 * half], ((1,), (0,)))
        down = dot(rows[1, :, :, at].reshape(slots, at.size), w[at, 2 * half :], ((1,), (0,)))
        if ch == 0:
            acc[:, 0 : 2 * half] = pre
            acc[:, 2 * half :] = down
        else:
            acc[:, 0 : 2 * half] += pre
            acc[:, 2 * half :] += down

    z_done = []
    chunks = len(in_spans)
    for step in range(chunks + 3):
        for lag, phase in enumerate((to_y, to_owner, to_partner, accumulate)):
            if 0 <= step - lag < chunks:
                phase(step - lag)

    @pl.loop(0, groups)
    def _(g):
        at = pl.ds(pl.multiple_of(g * HOT_CAP, HOT_CAP), HOT_CAP)
        gate = acc[at, 0:half]
        up = acc[at, half : 2 * half]
        d_hidden = acc[at, 2 * half :]
        sig = jax.nn.sigmoid(gate)
        active = gate * sig
        hid[at, :] = (active * up).astype(BF16)
        dab[at, 0:half] = (d_hidden * up * sig * (1.0 + gate * (1.0 - sig))).astype(BF16)
        dab[at, half:] = (d_hidden * active).astype(BF16)

    def results(ch):
        at = columns(out_spans[ch])
        part = dot(hid[...], w[at, 2 * half :], ((1,), (1,)))
        back = dot(dab[...], w[at, 0 : 2 * half], ((1,), (1,)))
        pair[0, :, :, at] = part.astype(BF16).reshape(groups, HOT_CAP, at.size)
        pair[1, :, :, at] = back.astype(BF16).reshape(groups, HOT_CAP, at.size)
        push(pair.at[1 - core, :, :, at], other.at[:, :, at], h_send.at[ch], h_recv.at[ch], partner)

    def to_origin(ch):
        at = columns(out_spans[ch])
        wait(other.at[:, :, at], h_recv.at[ch])
        total[:, :, at] = (pair[core, :, :, at].astype(F32) + other[:, :, at].astype(F32)).astype(BF16)
        place = ret.at[my_group, :, at]
        for step in range(1, groups):
            peer = g_peer(step)
            push(total.at[peer[0], :, at], place, r_send.at[ch], r_recv.at[ch], peer)
        pltpu.make_async_copy(total.at[my_group, :, at], place, r_recv.at[ch]).start()

    def weight_part(ch):
        at = columns(out_spans[ch])
        wg[0, at, 0 : 2 * half] = dot(
            rows[0, :, :, at].reshape(slots, at.size), dab[...], ((0,), (0,))
        ).astype(BF16)
        wg[0, at, 2 * half :] = dot(
            rows[1, :, :, at].reshape(slots, at.size), hid[...], ((0,), (0,))
        ).astype(BF16)

    def back_y(ch):
        at = columns(out_spans[ch])
        wait(ret.at[:, :, at], r_recv.at[ch])
        got = ret[:, :, at].reshape(slots, at.size)
        mixed = dot(spread[0], got, ((1,), (0,))) + dot(spread[1], got, ((1,), (0,)))
        res[:, :, :, at] = mixed.astype(BF16).reshape(ny, nz, 16, at.size)
        place = yrecv.at[y, :, :, at]
        for step in range(1, ny):
            push(
                res.at[(y + step) % ny, :, :, at], place, ry_send.at[ch], ry_recv.at[ch],
                y_peer(step),
            )
        pltpu.make_async_copy(res.at[y, :, :, at], place, ry_recv.at[ch]).start()

    def back_z(ch):
        at = columns(out_spans[ch])
        wait(yrecv.at[:, :, :, at], ry_recv.at[ch])
        ysum[:, :, at] = jnp.sum(yrecv[:, :, :, at].astype(F32), axis=0).astype(BF16)
        place = zrecv.at[z, :, at]
        for step in range(1, nz):
            push(
                ysum.at[(z + step) % nz, :, at], place, rz_send.at[ch], rz_recv.at[ch],
                z_peer(step, core),
            )
        pltpu.make_async_copy(ysum.at[z, :, at], place, rz_recv.at[ch]).start()

    def finish(ch):
        at = columns(out_spans[ch])
        wait(zrecv.at[:, :, at], rz_recv.at[ch])
        done = jnp.sum(zrecv[:, :, at].astype(F32), axis=0)
        fin[:, :, at] = done.reshape(2, 8, at.size).astype(BF16)
        place = out_ref.at[core, :, at]
        push(fin.at[1 - core, :, at], place, o_send.at[ch], o_recv.at[ch], partner)
        pltpu.make_async_copy(fin.at[core, :, at], place, o_recv.at[ch]).start()

    phases = (results, to_origin, weight_part, back_y, back_z, finish)
    chunks = len(out_spans)
    for step in range(chunks + len(phases) - 1):
        for lag, phase in enumerate(phases):
            if 0 <= step - lag < chunks:
                phase(step - lag)

    for ch, span in enumerate(z_spans):
        wait(buf.at[pl.ds(0, 2 * nz - 1), :, columns(span)], z_send.at[ch])
    for ch, span in enumerate(in_spans):
        at = columns(span)
        wait(buf.at[pl.ds(0, (ny - 1) * nz * 2), :, at], y_send.at[ch])
        wait(send.at[pl.ds(0, groups - 1), :, at], g_send.at[ch])
        wait(rows.at[core, :, :, at], f_send.at[ch])
    for ch, span in enumerate(out_spans):
        at = columns(span)
        wait(pair.at[1 - core, :, :, at], h_send.at[ch])
        wait(total.at[pl.ds(0, groups - 1), :, at], r_send.at[ch])
        wait(res.at[pl.ds(0, ny - 1), :, :, at], ry_send.at[ch])
        wait(ysum.at[pl.ds(0, nz - 1), :, at], rz_send.at[ch])
        wait(fin.at[1 - core, :, at], o_send.at[ch])
        wait(fin.at[:, :, at], o_recv.at[ch])


def shards(ny, nz, tokens, expert_ids, combine, hot_group, expert_weights, out_grad):
    groups = lax.axis_size("group")
    chips = ny * nz
    rows_here, model_width = tokens.shape
    group_len = expert_ids.shape[0]
    hidden3 = expert_weights.shape[2]
    half = hidden3 // 3
    slots = groups * HOT_CAP
    dma = pltpu.SemaphoreType.DMA
    block = (groups, HOT_CAP, model_width)
    hbm = pl.BlockSpec(memory_space=pltpu.HBM)
    vmem = pl.BlockSpec(memory_space=pltpu.VMEM)
    n_z, n_in, n_out = len(Z_CUTS), len(IN_CUTS), len(OUT_CUTS)
    out, weight_grad = pl.pallas_call(
        functools.partial(layer, groups, ny, nz),
        out_shape=(
            pltpu.VMEM((2, rows_here, model_width), BF16),
            pltpu.VMEM(expert_weights.shape, BF16),
        ),
        in_specs=[
            pl.BlockSpec(memory_space=pltpu.SMEM), vmem, vmem, hbm, hbm, hbm,
        ],
        out_specs=(vmem, vmem),
        scratch_shapes=[
            pltpu.VMEM((model_width, hidden3), BF16),
            pltpu.VMEM((2 * chips, rows_here, model_width), BF16),
            pltpu.VMEM(block, BF16),
            pltpu.VMEM((2,) + block, BF16),
            pltpu.VMEM((slots, group_len), BF16),
            pltpu.VMEM((slots, 128), F32),
            pltpu.VMEM((2, group_len, slots), BF16),
            pltpu.VMEM((slots, hidden3), F32),
            pltpu.VMEM((slots, half), BF16),
            pltpu.VMEM((slots, 2 * half), BF16),
            pltpu.VMEM((2,) + block, BF16),
            pltpu.VMEM(block, BF16),
            pltpu.VMEM(block, BF16),
            pltpu.VMEM(block, BF16),
            pltpu.VMEM((ny, nz, 16, model_width), BF16),
            pltpu.VMEM((ny, nz, 16, model_width), BF16),
            pltpu.VMEM((nz, 16, model_width), BF16),
            pltpu.VMEM((nz, 16, model_width), BF16),
            pltpu.VMEM((2, rows_here, model_width), BF16),
            dma,
        ]
        + [dma((n_z,))] * 2
        + [dma((n_in,))] * 6
        + [dma((n_out,))] * 10,
        compiler_params=pltpu.CompilerParams(
            collective_id=0, has_side_effects=True, vmem_limit_bytes=VMEM_BYTES
        ),
        cost_estimate=pl.CostEstimate(
            flops=6 * slots * model_width * hidden3, bytes_accessed=4 * model_width * hidden3,
            transcendentals=slots * half,
        ),
    )(hot_group, expert_ids.T, combine.T, tokens, out_grad, expert_weights)
    return out[0], out[1], weight_grad


def solution(mesh):
    nz = 4 if mesh.shape["member"] == 32 else 2
    ny = mesh.shape["member"] // (2 * nz)
    return jax.shard_map(
        functools.partial(shards, ny, nz),
        mesh=mesh,
        in_specs=(
            P(("group", "member"), None),
            P("group", None),
            P("group", None),
            P(),
            P(("group", "member"), None, None),
            P(("group", "member"), None),
        ),
        out_specs=(
            P(("group", "member"), None),
            P(("group", "member"), None),
            P(("group", "member"), None, None),
        ),
        check_vma=False,
    )
```

time: 90.5 us -> 82.6 us (0.913)
  local copies, waits for them, and re-layouts: 6.29 us -> 2.81 us
  Pallas kernels: 81.3 us -> 79 us
  other arithmetic: 2 us -> 0 us
    unnamed x1, local copies, waits for them, and re-layouts: 4.88 us -> 2.19 us
    pallas_call x1, Pallas kernels: 81.3 us -> 79 us  [shards(): pl.pallas_call(functools.partial(layer, groups, ny, nz), out_shape=(pltpu...]
    slice x1 -> x0, local copies, waits for them, and re-layouts: 1.4 us -> none  [shards(): return (out[0], out[1], weight_grad)]
    concatenate x1 -> x0, other arithmetic: 1.3 us -> none  [shards(): table = jnp.concatenate([expert_ids.astype(F32).T, combine.T], axis=0)]
where the time goes in v2:
time: 82.6 us; the launch traced here: 82.5 us
  Pallas kernels  79 us (96%)
  local copies, waits for them, and re-layouts  2.81 us (3%)
    pallas_call x1, Pallas kernels, shards(): pl.pallas_call(functools.partial(layer, groups, ny, nz), out_shape=(pltpu...  79 us
    unnamed x1, local copies, waits for them, and re-layouts  2.19 us

profile of v2, /device:TPU:1, one launch (start us, length us, event | category | flops | bytes accessed | tf_op | source)
XLA Modules:
  0.0 82.5 jit_solution(2447712075861601204)
XLA Ops:
  0.6 79.0 %shard_map.85 = (bf16[2,8,2048]{2,1,0:T(8,128)(2,1)S(1)}, bf16[1,2048,1152]{2,1,0:T(8,128)(2,1)S(1)}) custom-call(s32[16]{0:T(128)} %hot_ref.1, s32[8,256]{1,0:T(8,128)} %bitcast.6, f32[8,256]{1,0:T(8,128)} %bitcast.7, bf16[8,2048]{1,0:T(8,128)(2,1)} %tok_ref.1, bf16[8,2048]{1,0:T(8,128)(2,1)} %grad_ref.1, bf16[1,2048,1152]{2,1,0:T(8,128)(2,1)} %w_hbm.1), custom_call_target="tpu_custom_call" | custom-call | flops 5435817984 | bytes 9437184 | tf_op jit(solution)/shard_map/pallas_call | solution.py:300
  79.7 0.6 slice_bitcast_fusion
  80.3 2.2 %copy.10 = bf16[1,2048,1152]{2,1,0:T(8,128)(2,1)} copy(bf16[1,2048,1152]{2,1,0:T(8,128)(2,1)S(1)} %get-tuple-element.11) | data formatting | bytes 9437184

commit v3 on v2

--- a/solution.py
+++ b/solution.py
@@ -13,9 +13,13 @@
 CAP = 24
 HOT_CAP = 48
 VMEM_BYTES = 56 * 2**20
-Z_CUTS = (256, 512, 1280)
-IN_CUTS = (256, 512, 768, 512)
-OUT_CUTS = (256, 512, 512, 512, 256)
+Z_CUTS = (512, 512, 1024)
+IN_CUTS = (512, 512, 512, 512)
+LATE_CUTS = (1024, 1024)
+OUT_CUTS = (512, 512, 512, 512)
+Y_CUTS = (1024, 512, 512)
+FIRST = 32
+EARLY = 2
 
 
 def spans(cuts, width):
@@ -45,7 +49,14 @@
     model_width = tok_ref.shape[1]
     z_spans = spans(Z_CUTS, model_width)
     in_spans = spans(IN_CUTS, model_width)
+    late_spans = spans(LATE_CUTS, model_width)
     out_spans = spans(OUT_CUTS, model_width)
+    back_spans = spans(Y_CUTS, model_width)
+    both = ((0, FIRST), (FIRST, HOT_CAP))
+    in_items = [(both[0], span) for span in in_spans] + [(both[1], span) for span in late_spans]
+    out_items = [(both[0], span) for span in out_spans[:EARLY]]
+    out_items += [(both[1], (0, out_spans[EARLY - 1][1]))]
+    out_items += [((0, HOT_CAP), span) for span in out_spans[EARLY:]]
     top, tokens = ids_ref.shape
     slots = groups * HOT_CAP
     half = hid.shape[1]
@@ -86,6 +97,12 @@
 
     def columns(span):
         return pl.ds(span[0], span[1] - span[0])
+
+    def flat(part):
+        return pl.ds(part[0] * groups, (part[1] - part[0]) * groups)
+
+    def block_of(ref, part, span):
+        return ref[:, columns(part), columns(span)].reshape(flat(part).size, columns(span).size)
 
     for ch, span in enumerate(z_spans):
         cols = columns(span)
@@ -124,112 +141,137 @@
     spread_weight = jnp.where(is_rows, weight, 1.0)
     slot = lax.broadcasted_iota(jnp.int32, (HOT_CAP, tokens), 0).astype(F32)
     for g in range(groups):
-        at = pl.ds(g * HOT_CAP, HOT_CAP)
         one = jnp.where(rank[g : g + 1, :] == slot, 1.0, 0.0)
-        pick[at, :] = one.astype(BF16)
-        scale[at, :] = jnp.broadcast_to(
+        factor = jnp.broadcast_to(
             jnp.sum(one * gather_weight[g : g + 1, :], axis=1, keepdims=True), (HOT_CAP, 128)
         )
-        acc[at, 0:tokens] = one * spread_weight[g : g + 1, :]
+        spread_one = one * spread_weight[g : g + 1, :]
+        for low, high in both:
+            at = pl.ds(low * groups + g * (high - low), high - low)
+            pick[at, :] = one[low:high, :].astype(BF16)
+            scale[at, :] = factor[low:high, :]
+            acc[at, 0:tokens] = spread_one[low:high, :]
     turned = acc[:, 0:tokens].T
     spread[0] = turned.astype(BF16)
     spread[1] = (turned - turned.astype(BF16).astype(F32)).astype(BF16)
 
     def to_y(ch):
         mine = pl.ds(y * nz * 2, nz * 2)
-        first, last = in_spans[ch]
+        last = in_spans[ch][1]
         for zc, (a, b) in enumerate(z_spans):
-            if first < b <= last or (a < last <= b and b > last):
-                if zc not in z_done:
-                    z_done.append(zc)
-                    wait(buf.at[mine, :, columns((a, b))], z_recv.at[zc])
+            if a < last and zc not in z_done:
+                z_done.append(zc)
+                wait(buf.at[mine, :, columns((a, b))], z_recv.at[zc])
         block = buf.at[mine, :, columns(in_spans[ch])]
         for step in range(1, ny):
             push(block, block, y_send.at[ch], y_recv.at[ch], y_peer(step))
 
-    def to_owner(ch):
-        cols = columns(in_spans[ch])
-        wait(buf.at[pl.ds(0, (ny - 1) * nz * 2), :, cols], y_recv.at[ch])
+    def y_wait(ch):
+        wait(buf.at[pl.ds(0, (ny - 1) * nz * 2), :, columns(in_spans[ch])], y_recv.at[ch])
+
+    def to_owner(item):
+        part, span = in_items[item]
+        cols, slots_at, at = columns(span), columns(part), flat(part)
         width = cols.size
         block = buf[:, :, cols].astype(F32).reshape(tokens, width).astype(BF16)
-        picked = dot(pick[...], block, ((1,), (0,))) * scale[:, 0:1]
-        send[:, :, cols] = picked.astype(BF16).reshape(groups, HOT_CAP, width)
-        place = rows.at[core, my_group, :, cols]
+        picked = dot(pick[at, :], block, ((1,), (0,))) * scale[at, 0:1]
+        send[:, slots_at, cols] = picked.astype(BF16).reshape(groups, slots_at.size, width)
+        place = rows.at[core, my_group, slots_at, cols]
         for step in range(1, groups):
             peer = g_peer(step)
-            push(send.at[peer[0], :, cols], place, g_send.at[ch], g_recv.at[ch], peer)
-        pltpu.make_async_copy(send.at[my_group, :, cols], place, g_recv.at[ch]).start()
-
-    def to_partner(ch):
-        block = rows.at[core, :, :, columns(in_spans[ch])]
-        wait(block, g_recv.at[ch])
-        push(block, block, f_send.at[ch], f_recv.at[ch], partner)
-
-    def accumulate(ch):
-        at = columns(in_spans[ch])
-        wait(rows.at[1 - core, :, :, at], f_recv.at[ch])
-        if ch == 0:
+            push(send.at[peer[0], slots_at, cols], place, g_send.at[item], g_recv.at[item], peer)
+        pltpu.make_async_copy(send.at[my_group, slots_at, cols], place, g_recv.at[item]).start()
+
+    def to_partner(item):
+        part, span = in_items[item]
+        block = rows.at[core, :, columns(part), columns(span)]
+        wait(block, g_recv.at[item])
+        push(block, block, f_send.at[item], f_recv.at[item], partner)
+
+    def accumulate(item):
+        part, span = in_items[item]
+        at, to = columns(span), flat(part)
+        wait(rows.at[1 - core, :, columns(part), at], f_recv.at[item])
+        if item == 0:
             w_copy.wait()
-        pre = dot(rows[0, :, :, at].reshape(slots, at.size), w[at, 0 : 2 * half], ((1,), (0,)))
-        down = dot(rows[1, :, :, at].reshape(slots, at.size), w[at, 2 * half :], ((1,), (0,)))
-        if ch == 0:
-            acc[:, 0 : 2 * half] = pre
-            acc[:, 2 * half :] = down
+        pre = dot(block_of(rows.at[0], part, span), w[at, 0 : 2 * half], ((1,), (0,)))
+        down = dot(block_of(rows.at[1], part, span), w[at, 2 * half :], ((1,), (0,)))
+        if span[0] == 0:
+            acc[to, 0 : 2 * half] = pre
+            acc[to, 2 * half :] = down
         else:
-            acc[:, 0 : 2 * half] += pre
-            acc[:, 2 * half :] += down
-
-    z_done = []
-    chunks = len(in_spans)
-    for step in range(chunks + 3):
-        for lag, phase in enumerate((to_y, to_owner, to_partner, accumulate)):
-            if 0 <= step - lag < chunks:
-                phase(step - lag)
-
-    @pl.loop(0, groups)
-    def _(g):
-        at = pl.ds(pl.multiple_of(g * HOT_CAP, HOT_CAP), HOT_CAP)
-        gate = acc[at, 0:half]
-        up = acc[at, half : 2 * half]
-        d_hidden = acc[at, 2 * half :]
-        sig = jax.nn.sigmoid(gate)
-        active = gate * sig
-        hid[at, :] = (active * up).astype(BF16)
-        dab[at, 0:half] = (d_hidden * up * sig * (1.0 + gate * (1.0 - sig))).astype(BF16)
-        dab[at, half:] = (d_hidden * active).astype(BF16)
-
-    def results(ch):
-        at = columns(out_spans[ch])
-        part = dot(hid[...], w[at, 2 * half :], ((1,), (1,)))
-        back = dot(dab[...], w[at, 0 : 2 * half], ((1,), (1,)))
-        pair[0, :, :, at] = part.astype(BF16).reshape(groups, HOT_CAP, at.size)
-        pair[1, :, :, at] = back.astype(BF16).reshape(groups, HOT_CAP, at.size)
-        push(pair.at[1 - core, :, :, at], other.at[:, :, at], h_send.at[ch], h_recv.at[ch], partner)
-
-    def to_origin(ch):
-        at = columns(out_spans[ch])
-        wait(other.at[:, :, at], h_recv.at[ch])
-        total[:, :, at] = (pair[core, :, :, at].astype(F32) + other[:, :, at].astype(F32)).astype(BF16)
-        place = ret.at[my_group, :, at]
+            acc[to, 0 : 2 * half] += pre
+            acc[to, 2 * half :] += down
+
+    def activate(part):
+        size = part[1] - part[0]
+
+        @pl.loop(0, groups)
+        def _(g):
+            at = pl.ds(pl.multiple_of(part[0] * groups + g * size, 16), size)
+            gate = acc[at, 0:half]
+            up = acc[at, half : 2 * half]
+            d_hidden = acc[at, 2 * half :]
+            sig = jax.nn.sigmoid(gate)
+            active = gate * sig
+            hid[at, :] = (active * up).astype(BF16)
+            dab[at, 0:half] = (d_hidden * up * sig * (1.0 + gate * (1.0 - sig))).astype(BF16)
+            dab[at, half:] = (d_hidden * active).astype(BF16)
+
+    def results(item):
+        part, span = out_items[item]
+        at, to = columns(span), flat(part)
+        outs = (
+            dot(hid[to, :], w[at, 2 * half :], ((1,), (1,))).astype(BF16),
+            dot(dab[to, :], w[at, 0 : 2 * half], ((1,), (1,))).astype(BF16),
+        )
+        for kind, value in enumerate(outs):
+            for low, high in both:
+                if part[0] <= low and high <= part[1]:
+                    here = value[(low - part[0]) * groups : (high - part[0]) * groups, :]
+                    pair[kind, :, low:high, at] = here.reshape(groups, high - low, at.size)
+        rows_at = columns(part)
+        push(
+            pair.at[1 - core, :, rows_at, at], other.at[:, rows_at, at], h_send.at[item],
+            h_recv.at[item], partner,
+        )
+
+    def to_origin(item):
+        part, span = out_items[item]
+        at, rows_at = columns(span), columns(part)
+        wait(other.at[:, rows_at, at], h_recv.at[item])
+        total[:, rows_at, at] = (
+            pair[core, :, rows_at, at].astype(F32) + other[:, rows_at, at].astype(F32)
+        ).astype(BF16)
+        place = ret.at[my_group, rows_at, at]
         for step in range(1, groups):
             peer = g_peer(step)
-            push(total.at[peer[0], :, at], place, r_send.at[ch], r_recv.at[ch], peer)
-        pltpu.make_async_copy(total.at[my_group, :, at], place, r_recv.at[ch]).start()
+            push(total.at[peer[0], rows_at, at], place, r_send.at[item], r_recv.at[item], peer)
+        pltpu.make_async_copy(total.at[my_group, rows_at, at], place, r_recv.at[item]).start()
 
     def weight_part(ch):
-        at = columns(out_spans[ch])
-        wg[0, at, 0 : 2 * half] = dot(
-            rows[0, :, :, at].reshape(slots, at.size), dab[...], ((0,), (0,))
-        ).astype(BF16)
-        wg[0, at, 2 * half :] = dot(
-            rows[1, :, :, at].reshape(slots, at.size), hid[...], ((0,), (0,))
-        ).astype(BF16)
+        span = back_spans[ch]
+        at = columns(span)
+        for kind, grads, to in (
+            (0, dab, pl.ds(0, 2 * half)), (1, hid, pl.ds(2 * half, half)),
+        ):
+            wg[0, at, to] = sum(
+                dot(block_of(rows.at[kind], part, span), grads[flat(part), :], ((0,), (0,)))
+                for part in both
+            ).astype(BF16)
 
     def back_y(ch):
-        at = columns(out_spans[ch])
-        wait(ret.at[:, :, at], r_recv.at[ch])
-        got = ret[:, :, at].reshape(slots, at.size)
-        mixed = dot(spread[0], got, ((1,), (0,))) + dot(spread[1], got, ((1,), (0,)))
+        span = back_spans[ch]
+        at = columns(span)
+        for item, (part, (low, high)) in enumerate(out_items):
+            if low < span[1] and item not in arrived:
+                arrived.append(item)
+                wait(ret.at[:, columns(part), pl.ds(low, high - low)], r_recv.at[item])
+        mixed = sum(
+            dot(spread[piece, :, flat(part)], block_of(ret, part, span), ((1,), (0,)))
+            for part in both
+            for piece in range(2)
+        )
         res[:, :, :, at] = mixed.astype(BF16).reshape(ny, nz, 16, at.size)
         place = yrecv.at[y, :, :, at]
         for step in range(1, ny):
@@ -240,7 +282,7 @@
         pltpu.make_async_copy(res.at[y, :, :, at], place, ry_recv.at[ch]).start()
 
     def back_z(ch):
-        at = columns(out_spans[ch])
+        at = columns(back_spans[ch])
         wait(yrecv.at[:, :, :, at], ry_recv.at[ch])
         ysum[:, :, at] = jnp.sum(yrecv[:, :, :, at].astype(F32), axis=0).astype(BF16)
         place = zrecv.at[z, :, at]
@@ -252,7 +294,7 @@
         pltpu.make_async_copy(ysum.at[z, :, at], place, rz_recv.at[ch]).start()
 
     def finish(ch):
-        at = columns(out_spans[ch])
+        at = columns(back_spans[ch])
         wait(zrecv.at[:, :, at], rz_recv.at[ch])
         done = jnp.sum(zrecv[:, :, at].astype(F32), axis=0)
         fin[:, :, at] = done.reshape(2, 8, at.size).astype(BF16)
@@ -260,24 +302,66 @@
         push(fin.at[1 - core, :, at], place, o_send.at[ch], o_recv.at[ch], partner)
         pltpu.make_async_copy(fin.at[core, :, at], place, o_recv.at[ch]).start()
 
-    phases = (results, to_origin, weight_part, back_y, back_z, finish)
-    chunks = len(out_spans)
-    for step in range(chunks + len(phases) - 1):
-        for lag, phase in enumerate(phases):
-            if 0 <= step - lag < chunks:
-                phase(step - lag)
+    z_done, arrived = [], []
+    n_in, n_late, n_out, n_back = len(in_spans), len(late_spans), len(out_items), len(back_spans)
+    for step in range(n_in + 1):
+        if step < n_in:
+            to_y(step)
+        if step >= 1:
+            y_wait(step - 1)
+            to_owner(step - 1)
+        if step >= 3:
+            to_partner(step - 3)
+            if step >= 4:
+                accumulate(step - 4)
+    for late in range(n_late):
+        to_owner(n_in + late)
+    for item in range(max(n_in - 2, 0), n_in):
+        to_partner(item)
+        accumulate(item - 1)
+    accumulate(n_in - 1)
+    activate(both[0])
+    for item in range(EARLY):
+        results(item)
+        if item >= 1:
+            to_origin(item - 1)
+            if item - 1 < n_late:
+                to_partner(n_in + item - 1)
+    for late in range(EARLY - 1, n_late):
+        to_partner(n_in + late)
+    accumulate(n_in)
+    to_origin(EARLY - 1)
+    for late in range(1, n_late):
+        accumulate(n_in + late)
+    activate(both[1])
+    results(EARLY)
+    for item in range(EARLY + 1, n_out):
+        results(item)
+        to_origin(item - 1)
+    weight_part(0)
+    to_origin(n_out - 1)
+    for step in range(n_back + 2):
+        if step < n_back:
+            if step + 1 < n_back:
+                weight_part(step + 1)
+            back_y(step)
+        if 0 <= step - 1 < n_back:
+            back_z(step - 1)
+        if step >= 2:
+            finish(step - 2)
 
     for ch, span in enumerate(z_spans):
         wait(buf.at[pl.ds(0, 2 * nz - 1), :, columns(span)], z_send.at[ch])
     for ch, span in enumerate(in_spans):
+        wait(buf.at[pl.ds(0, (ny - 1) * nz * 2), :, columns(span)], y_send.at[ch])
+    for item, (part, span) in enumerate(in_items):
+        wait(send.at[pl.ds(0, groups - 1), columns(part), columns(span)], g_send.at[item])
+        wait(rows.at[core, :, columns(part), columns(span)], f_send.at[item])
+    for item, (part, span) in enumerate(out_items):
+        wait(pair.at[1 - core, :, columns(part), columns(span)], h_send.at[item])
+        wait(total.at[pl.ds(0, groups - 1), columns(part), columns(span)], r_send.at[item])
+    for ch, span in enumerate(back_spans):
         at = columns(span)
-        wait(buf.at[pl.ds(0, (ny - 1) * nz * 2), :, at], y_send.at[ch])
-        wait(send.at[pl.ds(0, groups - 1), :, at], g_send.at[ch])
-        wait(rows.at[core, :, :, at], f_send.at[ch])
-    for ch, span in enumerate(out_spans):
-        at = columns(span)
-        wait(pair.at[1 - core, :, :, at], h_send.at[ch])
-        wait(total.at[pl.ds(0, groups - 1), :, at], r_send.at[ch])
         wait(res.at[pl.ds(0, ny - 1), :, :, at], ry_send.at[ch])
         wait(ysum.at[pl.ds(0, nz - 1), :, at], rz_send.at[ch])
         wait(fin.at[1 - core, :, at], o_send.at[ch])
@@ -296,7 +380,8 @@
     block = (groups, HOT_CAP, model_width)
     hbm = pl.BlockSpec(memory_space=pltpu.HBM)
     vmem = pl.BlockSpec(memory_space=pltpu.VMEM)
-    n_z, n_in, n_out = len(Z_CUTS), len(IN_CUTS), len(OUT_CUTS)
+    n_z, n_y, n_in = len(Z_CUTS), len(IN_CUTS), len(IN_CUTS) + len(LATE_CUTS)
+    n_out, n_back = len(OUT_CUTS) + 1, len(Y_CUTS)
     out, weight_grad = pl.pallas_call(
         functools.partial(layer, groups, ny, nz),
         out_shape=(
@@ -330,8 +415,10 @@
             dma,
         ]
         + [dma((n_z,))] * 2
-        + [dma((n_in,))] * 6
-        + [dma((n_out,))] * 10,
+        + [dma((n_y,))] * 2
+        + [dma((n_in,))] * 4
+        + [dma((n_out,))] * 4
+        + [dma((n_back,))] * 6,
         compiler_params=pltpu.CompilerParams(
             collective_id=0, has_side_effects=True, vmem_limit_bytes=VMEM_BYTES
         ),

time: 82.6 us -> 78.9 us (0.955)
  Pallas kernels: 79 us -> 75.3 us
    pallas_call x1, Pallas kernels: 79 us -> 75.3 us  [shards(): pl.pallas_call(functools.partial(layer, groups, ny, nz), out_shape=(pltpu...]
where the time goes in v3:
time: 78.9 us; the launch traced here: 78.8 us
  Pallas kernels  75.3 us (95%)
  local copies, waits for them, and re-layouts  2.81 us (4%)
    pallas_call x1, Pallas kernels, shards(): pl.pallas_call(functools.partial(layer, groups, ny, nz), out_shape=(pltpu...  75.3 us
    unnamed x1, local copies, waits for them, and re-layouts  2.19 us

profile of v3, /device:TPU:1, one launch (start us, length us, event | category | flops | bytes accessed | tf_op | source)
XLA Modules:
  0.0 78.8 jit_solution(9792507346785024491)
XLA Ops:
  0.6 75.3 %shard_map.85 = (bf16[2,8,2048]{2,1,0:T(8,128)(2,1)S(1)}, bf16[1,2048,1152]{2,1,0:T(8,128)(2,1)S(1)}) custom-call(s32[16]{0:T(128)} %hot_ref.1, s32[8,256]{1,0:T(8,128)} %bitcast.6, f32[8,256]{1,0:T(8,128)} %bitcast.7, bf16[8,2048]{1,0:T(8,128)(2,1)} %tok_ref.1, bf16[8,2048]{1,0:T(8,128)(2,1)} %grad_ref.1, bf16[1,2048,1152]{2,1,0:T(8,128)(2,1)} %w_hbm.1), custom_call_target="tpu_custom_call" | custom-call | flops 5435817984 | bytes 9437184 | tf_op jit(solution)/shard_map/pallas_call | solution.py:385
  76.0 0.6 slice_bitcast_fusion
  76.6 2.2 %copy.10 = bf16[1,2048,1152]{2,1,0:T(8,128)(2,1)} copy(bf16[1,2048,1152]{2,1,0:T(8,128)(2,1)S(1)} %get-tuple-element.11) | data formatting | bytes 9437184

commit v4 on v3

--- a/solution.py
+++ b/solution.py
@@ -110,13 +110,13 @@
         sources = (tok_ref.at[:, cols], grad_ref.at[:, cols])
         for step in range(1, nz):
             for kind in range(2):
-                push(sources[kind], place, z_send.at[ch], z_recv.at[ch], z_peer(step, kind))
+                push(sources[kind], place, z_send, z_recv.at[ch], z_peer(step, kind))
         for kind in range(2):
 
             @pl.when(core == kind)
             def _():
                 pltpu.make_async_copy(sources[kind], place, z_recv.at[ch]).start()
-                push(sources[1 - kind], place, z_send.at[ch], z_recv.at[ch], partner)
+                push(sources[1 - kind], place, z_send, z_recv.at[ch], partner)
 
     ids = ids_ref[...]
     weights = weights_ref[...]
@@ -164,7 +164,7 @@
                 wait(buf.at[mine, :, columns((a, b))], z_recv.at[zc])
         block = buf.at[mine, :, columns(in_spans[ch])]
         for step in range(1, ny):
-            push(block, block, y_send.at[ch], y_recv.at[ch], y_peer(step))
+            push(block, block, y_send, y_recv.at[ch], y_peer(step))
 
     def y_wait(ch):
         wait(buf.at[pl.ds(0, (ny - 1) * nz * 2), :, columns(in_spans[ch])], y_recv.at[ch])
@@ -179,14 +179,14 @@
         place = rows.at[core, my_group, slots_at, cols]
         for step in range(1, groups):
             peer = g_peer(step)
-            push(send.at[peer[0], slots_at, cols], place, g_send.at[item], g_recv.at[item], peer)
+            push(send.at[peer[0], slots_at, cols], place, g_send, g_recv.at[item], peer)
         pltpu.make_async_copy(send.at[my_group, slots_at, cols], place, g_recv.at[item]).start()
 
     def to_partner(item):
         part, span = in_items[item]
         block = rows.at[core, :, columns(part), columns(span)]
         wait(block, g_recv.at[item])
-        push(block, block, f_send.at[item], f_recv.at[item], partner)
+        push(block, block, f_send, f_recv.at[item], partner)
 
     def accumulate(item):
         part, span = in_items[item]
@@ -232,7 +232,7 @@
                     pair[kind, :, low:high, at] = here.reshape(groups, high - low, at.size)
         rows_at = columns(part)
         push(
-            pair.at[1 - core, :, rows_at, at], other.at[:, rows_at, at], h_send.at[item],
+            pair.at[1 - core, :, rows_at, at], other.at[:, rows_at, at], h_send,
             h_recv.at[item], partner,
         )
 
@@ -246,7 +246,7 @@
         place = ret.at[my_group, rows_at, at]
         for step in range(1, groups):
             peer = g_peer(step)
-            push(total.at[peer[0], rows_at, at], place, r_send.at[item], r_recv.at[item], peer)
+            push(total.at[peer[0], rows_at, at], place, r_send, r_recv.at[item], peer)
         pltpu.make_async_copy(total.at[my_group, rows_at, at], place, r_recv.at[item]).start()
 
     def weight_part(ch):
@@ -276,7 +276,7 @@
         place = yrecv.at[y, :, :, at]
         for step in range(1, ny):
             push(
-                res.at[(y + step) % ny, :, :, at], place, ry_send.at[ch], ry_recv.at[ch],
+                res.at[(y + step) % ny, :, :, at], place, ry_send, ry_recv.at[ch],
                 y_peer(step),
             )
         pltpu.make_async_copy(res.at[y, :, :, at], place, ry_recv.at[ch]).start()
@@ -288,7 +288,7 @@
         place = zrecv.at[z, :, at]
         for step in range(1, nz):
             push(
-                ysum.at[(z + step) % nz, :, at], place, rz_send.at[ch], rz_recv.at[ch],
+                ysum.at[(z + step) % nz, :, at], place, rz_send, rz_recv.at[ch],
                 z_peer(step, core),
             )
         pltpu.make_async_copy(ysum.at[z, :, at], place, rz_recv.at[ch]).start()
@@ -299,40 +299,38 @@
         done = jnp.sum(zrecv[:, :, at].astype(F32), axis=0)
         fin[:, :, at] = done.reshape(2, 8, at.size).astype(BF16)
         place = out_ref.at[core, :, at]
-        push(fin.at[1 - core, :, at], place, o_send.at[ch], o_recv.at[ch], partner)
-        pltpu.make_async_copy(fin.at[core, :, at], place, o_recv.at[ch]).start()
+        push(fin.at[1 - core, :, at], place, o_send, o_recv, partner)
+        pltpu.make_async_copy(fin.at[core, :, at], place, o_recv).start()
 
     z_done, arrived = [], []
     n_in, n_late, n_out, n_back = len(in_spans), len(late_spans), len(out_items), len(back_spans)
-    for step in range(n_in + 1):
-        if step < n_in:
-            to_y(step)
-        if step >= 1:
-            y_wait(step - 1)
-            to_owner(step - 1)
-        if step >= 3:
-            to_partner(step - 3)
-            if step >= 4:
-                accumulate(step - 4)
-    for late in range(n_late):
-        to_owner(n_in + late)
-    for item in range(max(n_in - 2, 0), n_in):
-        to_partner(item)
-        accumulate(item - 1)
+    for ch in range(n_in):
+        to_y(ch)
+    for ch in range(n_in):
+        y_wait(ch)
+        to_owner(ch)
+        if ch == n_in - 1:
+            for late in range(n_late):
+                to_owner(n_in + late)
+        if ch >= 2:
+            to_partner(ch - 2)
+    for item in range(n_in - 2):
+        accumulate(item)
+    to_partner(n_in - 2)
+    to_partner(n_in - 1)
+    accumulate(n_in - 2)
     accumulate(n_in - 1)
     activate(both[0])
-    for item in range(EARLY):
+    results(0)
+    for item in range(1, EARLY):
         results(item)
-        if item >= 1:
-            to_origin(item - 1)
-            if item - 1 < n_late:
-                to_partner(n_in + item - 1)
-    for late in range(EARLY - 1, n_late):
+        to_origin(item - 1)
+    to_origin(EARLY - 1)
+    for late in range(n_late):
         to_partner(n_in + late)
-    accumulate(n_in)
-    to_origin(EARLY - 1)
-    for late in range(1, n_late):
-        accumulate(n_in + late)
+        if late >= 1:
+            accumulate(n_in + late - 1)
+    accumulate(n_in + n_late - 1)
     activate(both[1])
     results(EARLY)
     for item in range(EARLY + 1, n_out):
@@ -340,32 +338,25 @@
         to_origin(item - 1)
     weight_part(0)
     to_origin(n_out - 1)
-    for step in range(n_back + 2):
-        if step < n_back:
-            if step + 1 < n_back:
-                weight_part(step + 1)
-            back_y(step)
-        if 0 <= step - 1 < n_back:
-            back_z(step - 1)
-        if step >= 2:
-            finish(step - 2)
-
-    for ch, span in enumerate(z_spans):
-        wait(buf.at[pl.ds(0, 2 * nz - 1), :, columns(span)], z_send.at[ch])
-    for ch, span in enumerate(in_spans):
-        wait(buf.at[pl.ds(0, (ny - 1) * nz * 2), :, columns(span)], y_send.at[ch])
-    for item, (part, span) in enumerate(in_items):
-        wait(send.at[pl.ds(0, groups - 1), columns(part), columns(span)], g_send.at[item])
-        wait(rows.at[core, :, columns(part), columns(span)], f_send.at[item])
-    for item, (part, span) in enumerate(out_items):
-        wait(pair.at[1 - core, :, columns(part), columns(span)], h_send.at[item])
-        wait(total.at[pl.ds(0, groups - 1), columns(part), columns(span)], r_send.at[item])
-    for ch, span in enumerate(back_spans):
-        at = columns(span)
-        wait(res.at[pl.ds(0, ny - 1), :, :, at], ry_send.at[ch])
-        wait(ysum.at[pl.ds(0, nz - 1), :, at], rz_send.at[ch])
-        wait(fin.at[1 - core, :, at], o_send.at[ch])
-        wait(fin.at[:, :, at], o_recv.at[ch])
+    for ch in range(n_back):
+        if ch + 1 < n_back:
+            weight_part(ch + 1)
+        back_y(ch)
+    for ch in range(n_back):
+        back_z(ch)
+    for ch in range(n_back):
+        finish(ch)
+
+    wait(buf.at[pl.ds(0, 2 * nz - 1)], z_send)
+    wait(buf.at[pl.ds(0, (ny - 1) * nz * 2)], y_send)
+    wait(send.at[pl.ds(0, groups - 1)], g_send)
+    wait(rows.at[core], f_send)
+    wait(pair.at[1 - core], h_send)
+    wait(total.at[pl.ds(0, groups - 1)], r_send)
+    wait(res.at[pl.ds(0, ny - 1)], ry_send)
+    wait(ysum.at[pl.ds(0, nz - 1)], rz_send)
+    wait(fin.at[1 - core], o_send)
+    wait(fin, o_recv)
 
 
 def shards(ny, nz, tokens, expert_ids, combine, hot_group, expert_weights, out_grad):
@@ -414,11 +405,11 @@
             pltpu.VMEM((2, rows_here, model_width), BF16),
             dma,
         ]
-        + [dma((n_z,))] * 2
-        + [dma((n_y,))] * 2
-        + [dma((n_in,))] * 4
-        + [dma((n_out,))] * 4
-        + [dma((n_back,))] * 6,
+        + [dma, dma((n_z,)), dma, dma((n_y,))]
+        + [dma, dma((n_in,))] * 2
+        + [dma, dma((n_out,))] * 2
+        + [dma, dma((n_back,))] * 2
+        + [dma, dma],
         compiler_params=pltpu.CompilerParams(
             collective_id=0, has_side_effects=True, vmem_limit_bytes=VMEM_BYTES
         ),

time: 78.9 us -> 76.2 us (0.966)
  Pallas kernels: 75.3 us -> 72.6 us
    pallas_call x1, Pallas kernels: 75.3 us -> 72.6 us  [shards(): pl.pallas_call(functools.partial(layer, groups, ny, nz), out_shape=(pltpu...]
where the time goes in v4:
time: 76.2 us; the launch traced here: 76 us
  Pallas kernels  72.6 us (95%)
  local copies, waits for them, and re-layouts  2.81 us (4%)
    pallas_call x1, Pallas kernels, shards(): pl.pallas_call(functools.partial(layer, groups, ny, nz), out_shape=(pltpu...  72.6 us
    unnamed x1, local copies, waits for them, and re-layouts  2.19 us

profile of v4, /device:TPU:1, one launch (start us, length us, event | category | flops | bytes accessed | tf_op | source)
XLA Modules:
  0.0 76.0 jit_solution(13688337413287435617)
XLA Ops:
  0.6 72.6 %shard_map.85 = (bf16[2,8,2048]{2,1,0:T(8,128)(2,1)S(1)}, bf16[1,2048,1152]{2,1,0:T(8,128)(2,1)S(1)}) custom-call(s32[16]{0:T(128)} %hot_ref.1, s32[8,256]{1,0:T(8,128)} %bitcast.6, f32[8,256]{1,0:T(8,128)} %bitcast.7, bf16[8,2048]{1,0:T(8,128)(2,1)} %tok_ref.1, bf16[8,2048]{1,0:T(8,128)(2,1)} %grad_ref.1, bf16[1,2048,1152]{2,1,0:T(8,128)(2,1)} %w_hbm.1), custom_call_target="tpu_custom_call" | custom-call | flops 5435817984 | bytes 9437184 | tf_op jit(solution)/shard_map/pallas_call | solution.py:376
  73.2 0.6 slice_bitcast_fusion
  73.9 2.2 %copy.10 = bf16[1,2048,1152]{2,1,0:T(8,128)(2,1)} copy(bf16[1,2048,1152]{2,1,0:T(8,128)(2,1)S(1)} %get-tuple-element.11) | data formatting | bytes 9437184

commit v5 on v4

--- a/solution.py
+++ b/solution.py
@@ -13,11 +13,11 @@
 CAP = 24
 HOT_CAP = 48
 VMEM_BYTES = 56 * 2**20
-Z_CUTS = (512, 512, 1024)
+Z_CUTS = (512, 1536)
 IN_CUTS = (512, 512, 512, 512)
 LATE_CUTS = (1024, 1024)
 OUT_CUTS = (512, 512, 512, 512)
-Y_CUTS = (1024, 512, 512)
+Y_CUTS = (512, 512, 512, 512)
 FIRST = 32
 EARLY = 2
 
@@ -41,10 +41,9 @@
     hot_ref, ids_ref, weights_ref, tok_ref, grad_ref, w_hbm,
     out_ref, wg,
     w, buf, send, rows, pick, scale, spread, acc, hid, dab,
-    pair, other, total, ret, res, yrecv, ysum, zrecv, fin,
+    pair, other, total, ret, res, yrecv, ysum, zrecv,
     w_sem, z_send, z_recv, y_send, y_recv, g_send, g_recv, f_send, f_recv,
     h_send, h_recv, r_send, r_recv, ry_send, ry_recv, rz_send, rz_recv,
-    o_send, o_recv,
 ):
     model_width = tok_ref.shape[1]
     z_spans = spans(Z_CUTS, model_width)
@@ -284,23 +283,20 @@
     def back_z(ch):
         at = columns(back_spans[ch])
         wait(yrecv.at[:, :, :, at], ry_recv.at[ch])
-        ysum[:, :, at] = jnp.sum(yrecv[:, :, :, at].astype(F32), axis=0).astype(BF16)
-        place = zrecv.at[z, :, at]
+        summed = jnp.sum(yrecv[:, :, :, at].astype(F32), axis=0)
+        ysum[:, :, at] = summed.reshape(2 * nz, 8, at.size).astype(BF16)
+        place = zrecv.at[core, z, :, at]
         for step in range(1, nz):
-            push(
-                ysum.at[(z + step) % nz, :, at], place, rz_send, rz_recv.at[ch],
-                z_peer(step, core),
-            )
-        pltpu.make_async_copy(ysum.at[z, :, at], place, rz_recv.at[ch]).start()
+            for k in range(2):
+                piece = ysum.at[(z + step) % nz * 2 + k, :, at]
+                push(piece, place, rz_send, rz_recv.at[ch], z_peer(step, k))
+        push(ysum.at[2 * z + 1 - core, :, at], place, rz_send, rz_recv.at[ch], partner)
+        pltpu.make_async_copy(ysum.at[2 * z + core, :, at], place, rz_recv.at[ch]).start()
 
     def finish(ch):
         at = columns(back_spans[ch])
-        wait(zrecv.at[:, :, at], rz_recv.at[ch])
-        done = jnp.sum(zrecv[:, :, at].astype(F32), axis=0)
-        fin[:, :, at] = done.reshape(2, 8, at.size).astype(BF16)
-        place = out_ref.at[core, :, at]
-        push(fin.at[1 - core, :, at], place, o_send, o_recv, partner)
-        pltpu.make_async_copy(fin.at[core, :, at], place, o_recv).start()
+        wait(zrecv.at[:, :, :, at], rz_recv.at[ch])
+        out_ref[:, :, at] = jnp.sum(zrecv[:, :, :, at].astype(F32), axis=1).astype(BF16)
 
     z_done, arrived = [], []
     n_in, n_late, n_out, n_back = len(in_spans), len(late_spans), len(out_items), len(back_spans)
@@ -354,9 +350,7 @@
     wait(pair.at[1 - core], h_send)
     wait(total.at[pl.ds(0, groups - 1)], r_send)
     wait(res.at[pl.ds(0, ny - 1)], ry_send)
-    wait(ysum.at[pl.ds(0, nz - 1)], rz_send)
-    wait(fin.at[1 - core], o_send)
-    wait(fin, o_recv)
+    wait(ysum.at[pl.ds(0, 2 * nz - 1)], rz_send)
 
 
 def shards(ny, nz, tokens, expert_ids, combine, hot_group, expert_weights, out_grad):
@@ -400,16 +394,14 @@
             pltpu.VMEM(block, BF16),
             pltpu.VMEM((ny, nz, 16, model_width), BF16),
             pltpu.VMEM((ny, nz, 16, model_width), BF16),
-            pltpu.VMEM((nz, 16, model_width), BF16),
-            pltpu.VMEM((nz, 16, model_width), BF16),
-            pltpu.VMEM((2, rows_here, model_width), BF16),
+            pltpu.VMEM((2 * nz, 8, model_width), BF16),
+            pltpu.VMEM((2, nz, 8, model_width), BF16),
             dma,
         ]
         + [dma, dma((n_z,)), dma, dma((n_y,))]
         + [dma, dma((n_in,))] * 2
         + [dma, dma((n_out,))] * 2
-        + [dma, dma((n_back,))] * 2
-        + [dma, dma],
+        + [dma, dma((n_back,))] * 2,
         compiler_params=pltpu.CompilerParams(
             collective_id=0, has_side_effects=True, vmem_limit_bytes=VMEM_BYTES
         ),

time: 76.2 us -> 74.8 us (0.982)
  Pallas kernels: 72.6 us -> 71.3 us
    pallas_call x1, Pallas kernels: 72.6 us -> 71.3 us  [shards(): pl.pallas_call(functools.partial(layer, groups, ny, nz), out_shape=(pltpu...]
where the time goes in v5:
time: 74.8 us; the launch traced here: 74.7 us
  Pallas kernels  71.3 us (95%)
  local copies, waits for them, and re-layouts  2.81 us (4%)
    pallas_call x1, Pallas kernels, shards(): pl.pallas_call(functools.partial(layer, groups, ny, nz), out_shape=(pltpu...  71.3 us
    unnamed x1, local copies, waits for them, and re-layouts  2.19 us

profile of v5, /device:TPU:1, one launch (start us, length us, event | category | flops | bytes accessed | tf_op | source)
XLA Modules:
  0.0 74.7 jit_solution(8380899585727420462)
XLA Ops:
  0.6 71.3 %shard_map.85 = (bf16[2,8,2048]{2,1,0:T(8,128)(2,1)S(1)}, bf16[1,2048,1152]{2,1,0:T(8,128)(2,1)S(1)}) custom-call(s32[16]{0:T(128)} %hot_ref.1, s32[8,256]{1,0:T(8,128)} %bitcast.6, f32[8,256]{1,0:T(8,128)} %bitcast.7, bf16[8,2048]{1,0:T(8,128)(2,1)} %tok_ref.1, bf16[8,2048]{1,0:T(8,128)(2,1)} %grad_ref.1, bf16[1,2048,1152]{2,1,0:T(8,128)(2,1)} %w_hbm.1), custom_call_target="tpu_custom_call" | custom-call | flops 5435817984 | bytes 9437184 | tf_op jit(solution)/shard_map/pallas_call | solution.py:370
  71.9 0.6 slice_bitcast_fusion
  72.5 2.2 %copy.10 = bf16[1,2048,1152]{2,1,0:T(8,128)(2,1)} copy(bf16[1,2048,1152]{2,1,0:T(8,128)(2,1)S(1)} %get-tuple-element.11) | data formatting | bytes 9437184
